TPU v7x, 256 devices: a whole 4x4x8 slice. The times are simulated.
256 devices in a mesh: row: 16 (over y_hi, z), col: 16 (over y_lo, x, core).
Axes of the slice: x: 4, y: 4 (y_hi: 2, y_lo: 2; y = y_hi * 2 + y_lo), z: 8, core: 2. Of those that a mesh axis runs over, the one named last changes fastest.
Arguments:
- features: bfloat16 [65536, 256], P(('col', 'row')), may hold values from -6 to 6
- adj_tiles: bfloat16 [16, 512, 12, 128, 128], P('col', 'row'), may hold values from -0.0625 to 0.0625
- tile_cols: int32 [16, 512, 12], P('col', 'row'), may hold values from 0 to 31
- tile_count: int32 [16, 512], P('col', 'row'), may hold values from 1 to 12, as said below
- weight: bfloat16 [256, 256], replicated, may hold values from -0.375 to 0.375
- cotangent: bfloat16 [65536, 256], P(('row', 'col')), may hold values from -6 to 6
Outputs:
- activation: bfloat16 [65536, 256], P(('row', 'col'))
- feature_grad: bfloat16 [65536, 256], P(('col', 'row'))
Inputs may be any that keep to these rules, and one draw needn't show every extreme that they name: `tile_count`: some tile row of some block column has all 12 slots live; the number of live slots differs strongly between blocks.
All inputs are finite; a program needn't handle non-finite values.
Results may differ from a plain program's by a relative error of at most 0.0065.
Values may be sent and summed in bfloat16 or wider, within the bound.
No kernel may reach another device: no remote copies, remote signals or barrier semaphores. Data moves between devices by JAX's collectives and lax.ppermute only.
A program may use at most 128 MiB of HBM per device.

v0:
```python
import functools

import jax
import jax.numpy as jnp
from jax import lax
from jax.experimental import pallas as pl
from jax.experimental.pallas import tpu as pltpu
from jax.sharding import Mesh
from jax.sharding import PartitionSpec as P

BF = jnp.bfloat16
F32 = jnp.float32
SM = pl.BlockSpec(memory_space=pltpu.SMEM)
VM = pl.BlockSpec(memory_space=pltpu.VMEM)
ANY = pl.BlockSpec(memory_space=pl.ANY)
NZ, NY, NX = 8, 2, 4
TILE, F, SLOTS, TROWS, TCOLS = 128, 256, 12, 32, 32
HALF = TROWS // 2
WHOLE = 60 << 20
LARGE = 40 << 20
SMALL = 8 << 20


def shift(value, axis, size, step):
    return lax.ppermute(value, axis, [(i, (i + step) % size) for i in range(size)])


def swap(value, axis):
    return lax.ppermute(value, axis, [(0, 1), (1, 0)])


def plane_send(value, dy, dx):
    pairs = []
    for y in range(NY):
        for x in range(NX):
            pairs.append((y * NX + x, (y + dy) % NY * NX + (x + dx) % NX))
    return lax.ppermute(value, ("yl", "x"), pairs)


PLANE = [(dy, dx) for dy in range(NY) for dx in range(NX)]


def tile_row(u, core):
    return 4 * (u >> 1) + 2 * core + (u & 1)


def start_tiles(rows, tile_row_of, meta_ref, adj_ref, slab, sem):
    def each(u, act):
        t = tile_row_of(u)
        quads = (meta_ref[COUNTS_AT + t] + 3) >> 2
        for q in range(1, SLOTS // 4 + 1):

            @pl.when(quads == q)
            def _(q=q):
                live = pl.ds(0, 4 * q)
                act(pltpu.make_async_copy(adj_ref.at[t, live], slab.at[u, live], sem.at[u]))

    def start(u, carry):
        each(u, lambda copy: copy.start())
        return carry

    lax.fori_loop(0, rows, start, 0)
    return lambda u: each(u, lambda copy: copy.wait())


def gather_pieces(meta_ref, start, pieces, held):
    for k, piece in enumerate(pieces):
        held[pl.ds(meta_ref[start + k], piece.shape[0])] = piece[...]


COLS_AT, COUNTS_AT, PLACES_AT = 0, TROWS * SLOTS, TROWS * SLOTS + TROWS
GRADS_AT = PLACES_AT + 16
SENDS_AT = GRADS_AT + 16
CORE_AT = SENDS_AT + 16


def forward_body(meta_ref, adj_ref, *rest, n, first):
    pieces = rest[:n]
    core = meta_ref[CORE_AT]
    if first:
        out_ref, panel, slab, sem, piece_sem = rest[n:]
        core = 1 - core
        copies = []
        for piece in pieces:
            for i in range(piece.shape[0] // 2):
                k = len(copies)
                copies.append(
                    pltpu.make_async_copy(
                        piece.at[pl.ds(2 * i, 2)],
                        panel.at[pl.ds(meta_ref[PLACES_AT + k], 2)],
                        piece_sem.at[k],
                    )
                )
        for copy in copies:
            copy.start()
    else:
        out_ref, slab, sem = rest[n:]
        panel = pieces[0]
    arrived = start_tiles(HALF, lambda u: tile_row(u, core), meta_ref, adj_ref, slab, sem)
    if first:
        for copy in copies:
            copy.wait()

    def step(u, carry):
        arrived(u)
        t = tile_row(u, core)
        count = meta_ref[COUNTS_AT + t]
        pairs = (count + 1) >> 1
        for p in range(1, SLOTS // 2 + 1):

            @pl.when(pairs == p)
            def _(p=p):
                left = [slab[u, s] for s in range(2 * p)]
                left[-1] = jnp.where(count == 2 * p, left[-1], jnp.zeros_like(left[-1]))
                right = [panel[meta_ref[COLS_AT + t * SLOTS + s]] for s in range(2 * p)]
                out_ref[u] = jnp.dot(
                    jnp.concatenate(left, 1),
                    jnp.concatenate(right, 0),
                    preferred_element_type=F32,
                ).astype(out_ref.dtype)

        return carry

    lax.fori_loop(0, HALF, step, 0)


def forward(meta, adj, pieces):
    n = len(pieces)
    first = n > 1
    panel = [jax.ShapeDtypeStruct((TCOLS, TILE, F), BF)] if first else []
    return pl.pallas_call(
        functools.partial(forward_body, n=n, first=first),
        out_shape=[jax.ShapeDtypeStruct((HALF, TILE, F), BF if first else F32)] + panel,
        in_specs=[SM, ANY] + ([ANY] * n if first else [VM]),
        out_specs=[VM] * (1 + len(panel)),
        scratch_shapes=[
            pltpu.VMEM((HALF, SLOTS, TILE, TILE), BF),
            pltpu.SemaphoreType.DMA((HALF,)),
        ]
        + ([pltpu.SemaphoreType.DMA((TCOLS // 2,))] if first else []),
        compiler_params=pltpu.CompilerParams(vmem_limit_bytes=WHOLE if first else LARGE),
        cost_estimate=pl.CostEstimate(flops=4 * 10**9, bytes_accessed=9 << 20, transcendentals=0),
        name="forward",
    )(meta, adj, *pieces)


def backward_body(meta_ref, adj_ref, *rest, n):
    pieces = rest[:n]
    outs = rest[n : n + len(SENDS)]
    held, slab, sem, acc = rest[n + len(SENDS) :]
    arrived = start_tiles(TROWS, lambda t: t, meta_ref, adj_ref, slab, sem)
    gather_pieces(meta_ref, GRADS_AT, pieces, held)
    acc[...] = jnp.zeros_like(acc)

    def step(t, carry):
        arrived(t)
        count = meta_ref[COUNTS_AT + t]
        pairs = (count + 1) >> 1
        for p in range(1, SLOTS // 2 + 1):

            @pl.when(pairs == p)
            def _(p=p):
                grad = held[t]
                for q in range(p):
                    a0, a1 = slab[t, 2 * q], slab[t, 2 * q + 1]
                    if q == p - 1:
                        a1 = jnp.where(count == 2 * p, a1, jnp.zeros_like(a1))
                    terms = jnp.dot(grad, jnp.concatenate([a0, a1], 1), preferred_element_type=F32)
                    acc[meta_ref[COLS_AT + t * SLOTS + 2 * q]] += terms[:, :TILE]
                    acc[meta_ref[COLS_AT + t * SLOTS + 2 * q + 1]] += terms[:, TILE:]

        return carry

    lax.fori_loop(0, TROWS, step, 0)
    k = SENDS_AT
    for out, (steps, _) in zip(outs, SENDS):
        for j in range(len(steps)):
            for i in range(2):
                out[j, i] = acc[meta_ref[k] + i].astype(out.dtype)
            k += 1


SENDS = [((k, -k) if k in (1, 2, 3) else (k,), across) for across in (1, 0) for k in (4, 3, 2, 1, 0)]


def backward(meta, adj, pieces):
    n = len(pieces)
    return pl.pallas_call(
        functools.partial(backward_body, n=n),
        out_shape=[
            jax.ShapeDtypeStruct((len(steps), 2, F, TILE), BF if across else F32)
            for steps, across in SENDS
        ],
        in_specs=[SM, ANY] + [VM] * n,
        out_specs=[VM] * len(SENDS),
        scratch_shapes=[
            pltpu.VMEM((TROWS, F, TILE), BF),
            pltpu.VMEM((TROWS, SLOTS, TILE, TILE), BF),
            pltpu.SemaphoreType.DMA((TROWS,)),
            pltpu.VMEM((TCOLS, F, TILE), F32),
        ],
        compiler_params=pltpu.CompilerParams(vmem_limit_bytes=LARGE),
        cost_estimate=pl.CostEstimate(flops=8 * 10**9, bytes_accessed=18 << 20, transcendentals=0),
        name="backward",
    )(meta, adj, *pieces)


def pair_add_body(at_ref, mine_ref, other_ref, *outs):
    for k, out in enumerate(outs):
        rows = pl.ds(at_ref[k], 2)
        out[...] = (mine_ref[rows].astype(F32) + other_ref[rows].astype(F32)).astype(out.dtype)


def pair_add(at, mine, other):
    return pl.pallas_call(
        pair_add_body,
        out_shape=[jax.ShapeDtypeStruct((2, TILE, F), BF if any(to) else F32) for to in PLANE],
        in_specs=[SM, VM, VM],
        out_specs=[VM] * len(PLANE),
        compiler_params=pltpu.CompilerParams(vmem_limit_bytes=SMALL),
        name="pair_add",
    )(at, mine, other)


def middle_body(*refs):
    n = len(PLANE)
    pieces = refs[:n]
    weight_ref, cotangent_ref, act_ref, grad_ref = refs[n:]
    total = pieces[0][...].astype(F32)
    for piece in pieces[1:]:
        total = total + piece[...].astype(F32)
    aggregated = total.astype(BF).reshape(2 * TILE, F)
    weight = weight_ref[...]
    pre = jnp.dot(aggregated, weight, preferred_element_type=F32)
    sigma = jax.nn.sigmoid(pre)
    act_ref[...] = (pre * sigma).astype(BF)
    slope = sigma * (1.0 + pre * (1.0 - sigma))
    pre_grad = (cotangent_ref[...].astype(F32) * slope).astype(BF)
    grad = lax.dot_general(
        weight, pre_grad, (((1,), (1,)), ((), ())), preferred_element_type=F32
    ).astype(BF)
    grad_ref[0] = grad[:, :TILE]
    grad_ref[1] = grad[:, TILE:]


def middle(pieces, weight, cotangent):
    return pl.pallas_call(
        middle_body,
        out_shape=[
            jax.ShapeDtypeStruct((2 * TILE, F), BF),
            jax.ShapeDtypeStruct((2, F, TILE), BF),
        ],
        in_specs=[VM] * (len(pieces) + 2),
        out_specs=[VM, VM],
        compiler_params=pltpu.CompilerParams(vmem_limit_bytes=SMALL),
        name="middle",
    )(*pieces, weight, cotangent)


def finish_body(own_ref, far_ref, *rest):
    out_ref = rest[-1]
    for i in range(2):
        total = own_ref[0, i] + far_ref[0, i].astype(F32)
        for ref in rest[:-1]:
            total = total + ref[i].astype(F32)
        out_ref[pl.ds(i * TILE, TILE), :] = total.T.astype(BF)


def finish(*terms):
    return pl.pallas_call(
        finish_body,
        out_shape=jax.ShapeDtypeStruct((2 * TILE, F), BF),
        in_specs=[VM] * len(terms),
        out_specs=VM,
        compiler_params=pltpu.CompilerParams(vmem_limit_bytes=SMALL),
        name="finish",
    )(*terms)


def add(*terms):
    total = terms[0].astype(F32)
    for term in terms[1:]:
        total = total + term.astype(F32)
    return total.astype(BF)


def local(features, adj_tiles, tile_cols, tile_count, weight, cotangent):
    yh, z = lax.axis_index("yh"), lax.axis_index("z")
    yl, x, core = lax.axis_index("yl"), lax.axis_index("x"), lax.axis_index("c")

    adj = adj_tiles[0]
    own = features.reshape(2, TILE, F)
    pieces, places = [], []

    def keep(piece, half, *steps):
        pieces.append(piece)
        for step in steps:
            places.append(2 * (half * NZ + (z - step) % NZ))

    keep(own, yh, 0)
    keep(swap(own, "yh"), 1 - yh, 0)
    up = down = own
    for step in range(1, NZ // 2):
        up, down = shift(up, "z", NZ, 1), shift(down, "z", NZ, -1)
        both = jnp.concatenate([up, down], 0)
        keep(both, yh, step, -step)
        keep(swap(both, "yh"), 1 - yh, step, -step)
    up = shift(up, "z", NZ, 1)
    keep(up, yh, NZ // 2)
    keep(swap(up, "yh"), 1 - yh, NZ // 2)
    grad_at = [
        2 * (2 * ((yl - dy) % NY * NX + (x - dx) % NX) + side)
        for side in (core, 1 - core)
        for dy, dx in PLANE
    ]
    send = [
        2 * ((yh + across) % 2 * NZ + (z + step) % NZ) for steps, across in SENDS for step in steps
    ]
    meta = jnp.concatenate(
        [
            tile_cols[0].reshape(-1),
            tile_count[0].reshape(-1),
            jnp.stack(places + grad_at + send + [core]).astype(jnp.int32),
        ]
    )
    dests = jnp.stack([2 * ((yl + dy) % NY * NX + (x + dx) % NX) for dy, dx in PLANE]).astype(jnp.int32)

    for_other, panel = forward(meta, adj, pieces)
    theirs = swap(for_other, "c")
    (for_mine,) = forward(meta, adj, [panel])
    parts = pair_add(dests, for_mine, theirs)
    parts = [parts[0]] + [plane_send(part, dy, dx) for part, (dy, dx) in list(zip(parts, PLANE))[1:]]
    activation, grad = middle(parts, weight, cotangent)

    grads = [grad] + [plane_send(grad, dy, dx) for dy, dx in PLANE[1:]]
    grads_other = [swap(piece, "c") for piece in grads]
    far4, far3, far2, far1, far0, own4, own3, own2, own1, own0 = backward(
        meta, adj, grads + grads_other
    )

    far4, far3 = swap(far4, "yh"), swap(far3, "yh")
    up = shift(add(own4[0], far4[0]), "z", NZ, 1)
    far2, _ = lax.optimization_barrier((far2, far4))
    far2 = swap(far2, "yh")
    down = shift(add(own3[1], far3[1]), "z", NZ, -1)
    up = shift(add(own3[0], far3[0], up), "z", NZ, 1)
    far1, _ = lax.optimization_barrier((far1, far3))
    far1 = swap(far1, "yh")
    up = shift(add(own2[0], far2[0], up), "z", NZ, 1)
    down = shift(add(own2[1], far2[1], down), "z", NZ, -1)
    far0, _ = lax.optimization_barrier((far0, far2))
    far0 = swap(far0, "yh")
    up = shift(add(own1[0], far1[0], up), "z", NZ, 1)
    down = shift(add(own1[1], far1[1], down), "z", NZ, -1)
    feature_grad = finish(own0, far0, up, down)
    return activation, feature_grad


def solution(mesh):
    fine = Mesh(mesh.devices.reshape(2, NZ, NY, NX, 2), ("yh", "z", "yl", "x", "c"))
    row, col = ("yh", "z"), ("yl", "x", "c")
    in_specs = (
        P(col + row, None),
        P(col, row, None, None, None),
        P(col, row, None),
        P(col, row),
        P(),
        P(row + col, None),
    )
    out_specs = (P(row + col, None), P(col + row, None))
    return jax.shard_map(local, mesh=fine, in_specs=in_specs, out_specs=out_specs, check_vma=False)
```

profile of v0, /device:TPU:8, one launch (start us, length us, event | category | flops | bytes accessed | tf_op | source)
XLA Modules:
  0.0 145.7 jit_solution(975149673997908156)
XLA Ops:
  0.6 2.0 %collective-permute-start.1 = (bf16[2,128,256]{2,1,0:T(8,128)(2,1)}, bf16[2,128,256]{2,1,0:T(8,128)(2,1)S(1)}, u32[]{:S(2)}, u32[]{:S(2)}) collective-permute-start(bf16[2,128,256]{2,1,0:T(8,128)(2,1)} %bitcast.88), channel_id=1, source_target_pairs={{0,16},{16,32},{32,48},{48,64},{64,80},{80,96},{96,112},{112,0},{1... | collective-permute-start | bytes 393224 | tf_op jit(solution)/shard_map/ppermute | solution.py:25
  2.6 4.0 %collective-permute-start.2 = (bf16[2,128,256]{2,1,0:T(8,128)(2,1)}, bf16[2,128,256]{2,1,0:T(8,128)(2,1)S(1)}, u32[]{:S(2)}, u32[]{:S(2)}) collective-permute-start(bf16[2,128,256]{2,1,0:T(8,128)(2,1)} %bitcast.89), channel_id=1, source_target_pairs={{0,112},{16,0},{32,16},{48,32},{64,48},{80,64},{96,80},{112,96},{1... | collective-permute-start | bytes 393224 | tf_op jit(solution)/shard_map/ppermute | solution.py:25
  6.7 3.6 %collective-permute-done.1 = bf16[2,128,256]{2,1,0:T(8,128)(2,1)S(1)} collective-permute-done((bf16[2,128,256]{2,1,0:T(8,128)(2,1)}, bf16[2,128,256]{2,1,0:T(8,128)(2,1)S(1)}, u32[]{:S(2)}, u32[]{:S(2)}) %collective-permute-start.1) | collective-permute-done | bytes 131104 | tf_op jit(solution)/shard_map/ppermute | solution.py:25
  10.3 3.3 %collective-permute-start.5 = (bf16[2,128,256]{2,1,0:T(8,128)(2,1)S(1)}, bf16[2,128,256]{2,1,0:T(8,128)(2,1)S(1)}, u32[]{:S(2)}, u32[]{:S(2)}) collective-permute-start(bf16[2,128,256]{2,1,0:T(8,128)(2,1)S(1)} %collective-permute-done.2), channel_id=1, source_target_pairs={{0,112},{16,0},{32,16},{48,32},{64,48},{80,64},{96,80},{112,96},{1... | collective-permute-start | bytes 393224 | tf_op jit(solution)/shard_map/ppermute | solution.py:25
  13.7 2.4 %collective-permute-start.3 = (bf16[4,128,256]{2,1,0:T(8,128)(2,1)S(1)}, bf16[4,128,256]{2,1,0:T(8,128)(2,1)S(1)}, u32[]{:S(2)}, u32[]{:S(2)}) collective-permute-start(bf16[4,128,256]{2,1,0:T(8,128)(2,1)S(1)} %constant_dynamic-update-slice_fusion.rest_2_), channel_id=1, source_target_pairs={{0,128},{128,0},{1,129},{129,1},{2,130},{130,2},{3,131},{131,3},{4... | collective-permute-start | bytes 786440 | tf_op jit(solution)/shard_map/ppermute | solution.py:29
  16.5 3.3 %collective-permute-start.8 = (bf16[2,128,256]{2,1,0:T(8,128)(2,1)S(1)}, bf16[2,128,256]{2,1,0:T(8,128)(2,1)S(1)}, u32[]{:S(2)}, u32[]{:S(2)}) collective-permute-start(bf16[2,128,256]{2,1,0:T(8,128)(2,1)S(1)} %collective-permute-done.5), channel_id=1, source_target_pairs={{0,112},{16,0},{32,16},{48,32},{64,48},{80,64},{96,80},{112,96},{1... | collective-permute-start | bytes 393224 | tf_op jit(solution)/shard_map/ppermute | solution.py:25
  19.8 2.4 %collective-permute-start.6 = (bf16[4,128,256]{2,1,0:T(8,128)(2,1)S(1)}, bf16[4,128,256]{2,1,0:T(8,128)(2,1)S(1)}, u32[]{:S(2)}, u32[]{:S(2)}) collective-permute-start(bf16[4,128,256]{2,1,0:T(8,128)(2,1)S(1)} %constant_dynamic-update-slice_fusion.2.rest_4_), channel_id=1, source_target_pairs={{0,128},{128,0},{1,129},{129,1},{2,130},{130,2},{3,131},{131,3},{4... | collective-permute-start | bytes 786440 | tf_op jit(solution)/shard_map/ppermute | solution.py:29
  22.7 2.4 %collective-permute-start.9 = (bf16[4,128,256]{2,1,0:T(8,128)(2,1)S(1)}, bf16[4,128,256]{2,1,0:T(8,128)(2,1)S(1)}, u32[]{:S(2)}, u32[]{:S(2)}) collective-permute-start(bf16[4,128,256]{2,1,0:T(8,128)(2,1)S(1)} %constant_dynamic-update-slice_fusion.4.rest_6_), channel_id=1, source_target_pairs={{0,128},{128,0},{1,129},{129,1},{2,130},{130,2},{3,131},{131,3},{4... | collective-permute-start | bytes 786440 | tf_op jit(solution)/shard_map/ppermute | solution.py:29
  26.3 2.5 %collective-permute-done.10.rest_8_ = bf16[2,128,256]{2,1,0:T(8,128)(2,1)S(1)} collective-permute-done((bf16[2,128,256]{2,1,0:T(8,128)(2,1)S(1)}, bf16[2,128,256]{2,1,0:T(8,128)(2,1)S(1)}, u32[]{:S(2)}, u32[]{:S(2)}) %collective-permute-start.10) | collective-permute-done | bytes 131104 | tf_op jit(solution)/shard_map/ppermute | solution.py:25
  28.8 2.3 %collective-permute-start.11 = (bf16[2,128,256]{2,1,0:T(8,128)(2,1)S(1)}, bf16[2,128,256]{2,1,0:T(8,128)(2,1)S(1)}, u32[]{:S(2)}, u32[]{:S(2)}) collective-permute-start(bf16[2,128,256]{2,1,0:T(8,128)(2,1)S(1)} %collective-permute-done.10.rest_8_), channel_id=1, source_target_pairs={{0,128},{128,0},{1,129},{129,1},{2,130},{130,2},{3,131},{131,3},{4... | collective-permute-start | bytes 393224 | tf_op jit(solution)/shard_map/ppermute | solution.py:29
  32.1 5.6 %collective-permute-done.rest_1_ = bf16[2,128,256]{2,1,0:T(8,128)(2,1)S(1)} collective-permute-done((bf16[2,128,256]{2,1,0:T(8,128)(2,1)}, bf16[2,128,256]{2,1,0:T(8,128)(2,1)S(1)}, u32[]{:S(2)}, u32[]{:S(2)}) %collective-permute-start) | collective-permute-done | bytes 131104 | tf_op jit(solution)/shard_map/ppermute | solution.py:29
  39.8 8.9 %forward.2 = (bf16[16,128,256]{2,1,0:T(8,128)(2,1)}, bf16[32,128,256]{2,1,0:T(8,128)(2,1)}) custom-call(s32[465]{0:T(512)} %concatenate.12.meta_ref, bf16[32,12,128,128]{3,2,1,0:T(8,128)(2,1)} %bitcast.84, bf16[2,128,256]{2,1,0:T(8,128)(2,1)} %bitcast.91, bf16[2,128,256]{2,1,0:T(8,128)(2,1)} %copy-done.13, bf16[4,128,256]{2,1,0:T(8,128)(2,1)} %copy-done.5, ...), custom_call_target="tpu_custom_call" | custom-call | flops 4000000000 | bytes 9437184 | tf_op jit(solution)/shard_map/forward/pallas_call | solution.py:131
  49.0 1.6 %copy-done = bf16[32,128,256]{2,1,0:T(8,128)(2,1)S(1)} copy-done((bf16[32,128,256]{2,1,0:T(8,128)(2,1)S(1)}, bf16[32,128,256]{2,1,0:T(8,128)(2,1)}, u32[]{:S(2)}) %copy-start) | copy-done | bytes 2097176
  50.6 5.9 %forward.3.mine_ref = f32[16,128,256]{2,1,0:T(8,128)S(1)} custom-call(s32[465]{0:T(512)S(1)} %copy-done.3, bf16[32,12,128,128]{3,2,1,0:T(8,128)(2,1)} %bitcast.85, bf16[32,128,256]{2,1,0:T(8,128)(2,1)S(1)} %copy-done), custom_call_target="tpu_custom_call" | custom-call | flops 4000000000 | bytes 9437184 | tf_op jit(solution)/shard_map/forward/pallas_call | solution.py:131
  57.4 2.8 %collective-permute-start.14 = (bf16[2,128,256]{2,1,0:T(8,128)(2,1)S(1)}, bf16[2,128,256]{2,1,0:T(8,128)(2,1)S(1)}, u32[]{:S(2)}, u32[]{:S(2)}) collective-permute-start(bf16[2,128,256]{2,1,0:T(8,128)(2,1)S(1)} %get-tuple-element.31), channel_id=1, source_target_pairs={{0,4},{2,6},{4,0},{6,2},{8,12},{10,14},{12,8},{14,10},{1,5},{3,7},... | collective-permute-start | bytes 393224 | tf_op jit(solution)/shard_map/ppermute | solution.py:37
  63.8 3.8 %collective-permute-done.13.refs_1_ = bf16[2,128,256]{2,1,0:T(8,128)(2,1)S(1)} collective-permute-done((bf16[2,128,256]{2,1,0:T(8,128)(2,1)S(1)}, bf16[2,128,256]{2,1,0:T(8,128)(2,1)S(1)}, u32[]{:S(2)}, u32[]{:S(2)}) %collective-permute-start.13) | collective-permute-done | bytes 131104 | tf_op jit(solution)/shard_map/ppermute | solution.py:37
  68.6 3.1 %collective-permute-done.17.refs_5_ = bf16[2,128,256]{2,1,0:T(8,128)(2,1)S(1)} collective-permute-done((bf16[2,128,256]{2,1,0:T(8,128)(2,1)S(1)}, bf16[2,128,256]{2,1,0:T(8,128)(2,1)S(1)}, u32[]{:S(2)}, u32[]{:S(2)}) %collective-permute-start.17) | collective-permute-done | bytes 131104 | tf_op jit(solution)/shard_map/ppermute | solution.py:37
  71.7 4.7 %collective-permute-done.18.refs_6_ = bf16[2,128,256]{2,1,0:T(8,128)(2,1)S(1)} collective-permute-done((bf16[2,128,256]{2,1,0:T(8,128)(2,1)S(1)}, bf16[2,128,256]{2,1,0:T(8,128)(2,1)S(1)}, u32[]{:S(2)}, u32[]{:S(2)}) %collective-permute-start.18) | collective-permute-done | bytes 131104 | tf_op jit(solution)/shard_map/ppermute | solution.py:37
  78.0 2.2 %collective-permute-start.25 = (bf16[2,256,128]{2,1,0:T(8,128)(2,1)S(1)}, bf16[2,256,128]{2,1,0:T(8,128)(2,1)S(1)}, u32[]{:S(2)}, u32[]{:S(2)}) collective-permute-start(bf16[2,256,128]{2,1,0:T(8,128)(2,1)S(1)} %get-tuple-element.38.rest_0_), channel_id=1, source_target_pairs={{0,12},{2,14},{4,8},{6,10},{8,4},{10,6},{12,0},{14,2},{1,13},{3,15... | collective-permute-start | bytes 393224 | tf_op jit(solution)/shard_map/ppermute | solution.py:37
  82.4 2.6 %collective-permute-start.22 = (bf16[2,256,128]{2,1,0:T(8,128)(2,1)S(1)}, bf16[2,256,128]{2,1,0:T(8,128)(2,1)S(1)}, u32[]{:S(2)}, u32[]{:S(2)}) collective-permute-start(bf16[2,256,128]{2,1,0:T(8,128)(2,1)S(1)} %get-tuple-element.38.rest_0_), channel_id=1, source_target_pairs={{0,6},{2,0},{4,2},{6,4},{8,14},{10,8},{12,10},{14,12},{1,7},{3,1},... | collective-permute-start | bytes 393224 | tf_op jit(solution)/shard_map/ppermute | solution.py:37
  87.2 1.9 %collective-permute-start.20 = (bf16[2,256,128]{2,1,0:T(8,128)(2,1)S(1)}, bf16[2,256,128]{2,1,0:T(8,128)(2,1)S(1)}, u32[]{:S(2)}, u32[]{:S(2)}) collective-permute-start(bf16[2,256,128]{2,1,0:T(8,128)(2,1)S(1)} %get-tuple-element.38.rest_0_), channel_id=1, source_target_pairs={{0,2},{2,4},{4,6},{6,0},{8,10},{10,12},{12,14},{14,8},{1,3},{3,5},... | collective-permute-start | bytes 393224 | tf_op jit(solution)/shard_map/ppermute | solution.py:37
  90.4 2.2 %collective-permute-done.23.rest_4_ = bf16[2,256,128]{2,1,0:T(8,128)(2,1)S(1)} collective-permute-done((bf16[2,256,128]{2,1,0:T(8,128)(2,1)S(1)}, bf16[2,256,128]{2,1,0:T(8,128)(2,1)S(1)}, u32[]{:S(2)}, u32[]{:S(2)}) %collective-permute-start.23) | collective-permute-done | bytes 131104 | tf_op jit(solution)/shard_map/ppermute | solution.py:37
  93.2 2.2 %collective-permute-done.20.rest_1_ = bf16[2,256,128]{2,1,0:T(8,128)(2,1)S(1)} collective-permute-done((bf16[2,256,128]{2,1,0:T(8,128)(2,1)S(1)}, bf16[2,256,128]{2,1,0:T(8,128)(2,1)S(1)}, u32[]{:S(2)}, u32[]{:S(2)}) %collective-permute-start.20) | collective-permute-done | bytes 131104 | tf_op jit(solution)/shard_map/ppermute | solution.py:37
  97.3 13.1 %backward.1 = (bf16[1,2,256,128]{3,2,1,0:T(8,128)(2,1)S(1)}, bf16[2,2,256,128]{3,2,1,0:T(8,128)(2,1)S(1)}, bf16[2,2,256,128]{3,2,1,0:T(8,128)(2,1)S(1)}, bf16[2,...) custom-call(s32[465]{0:T(512)S(1)} %copy-done.3, ...), custom_call_target="tpu_custom_call" | custom-call | flops 8000000000 | bytes 18874368 | tf_op jit(solution)/shard_map/backward/pallas_call | solution.py:188
  110.7 3.2 %collective-permute-start.38 = (bf16[2,2,256,128]{3,2,1,0:T(8,128)(2,1)S(1)}, bf16[2,2,256,128]{3,2,1,0:T(8,128)(2,1)S(1)}, u32[]{:S(2)}, u32[]{:S(2)}) collective-permute-start(bf16[2,2,256,128]{3,2,1,0:T(8,128)(2,1)S(1)} %get-tuple-element.47), channel_id=1, source_target_pairs={{0,128},{128,0},{1,129},{129,1},{2,130},{130,2},{3,131},{131,3},{4... | collective-permute-start | bytes 786440 | tf_op jit(solution)/shard_map/ppermute | solution.py:29
  114.0 4.3 %collective-permute-done.35 = bf16[1,2,256,128]{3,2,1,0:T(8,128)(2,1)S(1)} collective-permute-done((bf16[1,2,256,128]{3,2,1,0:T(8,128)(2,1)S(1)}, bf16[1,2,256,128]{3,2,1,0:T(8,128)(2,1)S(1)}, u32[]{:S(2)}, u32[]{:S(2)}) %collective-permute-start.35) | collective-permute-done | bytes 131104 | tf_op jit(solution)/shard_map/ppermute | solution.py:29
  118.6 5.4 %collective-permute-done.38 = bf16[2,2,256,128]{3,2,1,0:T(8,128)(2,1)S(1)} collective-permute-done((bf16[2,2,256,128]{3,2,1,0:T(8,128)(2,1)S(1)}, bf16[2,2,256,128]{3,2,1,0:T(8,128)(2,1)S(1)}, u32[]{:S(2)}, u32[]{:S(2)}) %collective-permute-start.38) | collective-permute-done | bytes 262176 | tf_op jit(solution)/shard_map/ppermute | solution.py:29
  127.0 2.2 %collective-permute-done.36 = bf16[2,2,256,128]{3,2,1,0:T(8,128)(2,1)S(1)} collective-permute-done((bf16[2,2,256,128]{3,2,1,0:T(8,128)(2,1)S(1)}, bf16[2,2,256,128]{3,2,1,0:T(8,128)(2,1)S(1)}, u32[]{:S(2)}, u32[]{:S(2)}) %collective-permute-start.36) | collective-permute-done | bytes 262176 | tf_op jit(solution)/shard_map/ppermute | solution.py:29
  129.2 1.7 %collective-permute-done.41 = bf16[2,256,128]{2,1,0:T(8,128)(2,1)S(1)} collective-permute-done((bf16[2,256,128]{2,1,0:T(8,128)(2,1)S(1)}, bf16[2,256,128]{2,1,0:T(8,128)(2,1)S(1)}, u32[]{:S(2)}, u32[]{:S(2)}) %collective-permute-start.41) | collective-permute-done | bytes 131104 | tf_op jit(solution)/shard_map/ppermute | solution.py:25
  131.1 2.0 %collective-permute-start.42 = (bf16[2,256,128]{2,1,0:T(8,128)(2,1)S(1)}, bf16[2,256,128]{2,1,0:T(8,128)(2,1)S(1)}, u32[]{:S(2)}, u32[]{:S(2)}) collective-permute-start(bf16[2,256,128]{2,1,0:T(8,128)(2,1)S(1)} %get-tuple-element.55), channel_id=1, source_target_pairs={{0,16},{16,32},{32,48},{48,64},{64,80},{80,96},{96,112},{112,0},{1... | collective-permute-start | bytes 393224 | tf_op jit(solution)/shard_map/ppermute | solution.py:25
  139.7 2.9 %collective-permute-done.46.rest_1_ = bf16[2,256,128]{2,1,0:T(8,128)(2,1)S(1)} collective-permute-done((bf16[2,256,128]{2,1,0:T(8,128)(2,1)S(1)}, bf16[2,256,128]{2,1,0:T(8,128)(2,1)S(1)}, u32[]{:S(2)}, u32[]{:S(2)}) %collective-permute-start.46) | collective-permute-done | bytes 131104 | tf_op jit(solution)/shard_map/ppermute | solution.py:25
  142.7 2.3 %collective-permute-done.43.rest_0_ = bf16[2,256,128]{2,1,0:T(8,128)(2,1)S(1)} collective-permute-done((bf16[2,256,128]{2,1,0:T(8,128)(2,1)S(1)}, bf16[2,256,128]{2,1,0:T(8,128)(2,1)S(1)}, u32[]{:S(2)}, u32[]{:S(2)}) %collective-permute-start.43) | collective-permute-done | bytes 131104 | tf_op jit(solution)/shard_map/ppermute | solution.py:25
  (113 shorter events, 31.9 us)
Async XLA Ops:
  0.6 9.6 %collective-permute-start.1 = (bf16[2,128,256]{2,1,0:T(8,128)(2,1)}, bf16[2,128,256]{2,1,0:T(8,128)(2,1)S(1)}, u32[]{:S(2)}, u32[]{:S(2)}) collective-permute-start(bf16[2,128,256]{2,1,0:T(8,128)(2,1)} %bitcast.88), channel_id=1, source_target_pairs={{0,16},{16,32},{32,48},{48,64},{64,80},{80,96},{96,112},{112,0},{1... | collective-permute-start | bytes 393224 | tf_op jit(solution)/shard_map/ppermute | solution.py:25
  2.6 7.7 %collective-permute-start.2 = (bf16[2,128,256]{2,1,0:T(8,128)(2,1)}, bf16[2,128,256]{2,1,0:T(8,128)(2,1)S(1)}, u32[]{:S(2)}, u32[]{:S(2)}) collective-permute-start(bf16[2,128,256]{2,1,0:T(8,128)(2,1)} %bitcast.89), channel_id=1, source_target_pairs={{0,112},{16,0},{32,16},{48,32},{64,48},{80,64},{96,80},{112,96},{1... | collective-permute-start | bytes 393224 | tf_op jit(solution)/shard_map/ppermute | solution.py:25
  10.3 6.2 %collective-permute-start.4 = (bf16[2,128,256]{2,1,0:T(8,128)(2,1)S(1)}, bf16[2,128,256]{2,1,0:T(8,128)(2,1)S(1)}, u32[]{:S(2)}, u32[]{:S(2)}) collective-permute-start(bf16[2,128,256]{2,1,0:T(8,128)(2,1)S(1)} %collective-permute-done.1), channel_id=1, source_target_pairs={{0,16},{16,32},{32,48},{48,64},{64,80},{80,96},{96,112},{112,0},{1... | collective-permute-start | bytes 393224 | tf_op jit(solution)/shard_map/ppermute | solution.py:25
  13.7 24.0 %collective-permute-start.3 = (bf16[4,128,256]{2,1,0:T(8,128)(2,1)S(1)}, bf16[4,128,256]{2,1,0:T(8,128)(2,1)S(1)}, u32[]{:S(2)}, u32[]{:S(2)}) collective-permute-start(bf16[4,128,256]{2,1,0:T(8,128)(2,1)S(1)} %constant_dynamic-update-slice_fusion.rest_2_), channel_id=1, source_target_pairs={{0,128},{128,0},{1,129},{129,1},{2,130},{130,2},{3,131},{131,3},{4... | collective-permute-start | bytes 786440 | tf_op jit(solution)/shard_map/ppermute | solution.py:29
  16.5 6.2 %collective-permute-start.7 = (bf16[2,128,256]{2,1,0:T(8,128)(2,1)S(1)}, bf16[2,128,256]{2,1,0:T(8,128)(2,1)S(1)}, u32[]{:S(2)}, u32[]{:S(2)}) collective-permute-start(bf16[2,128,256]{2,1,0:T(8,128)(2,1)S(1)} %collective-permute-done.4), channel_id=1, source_target_pairs={{0,16},{16,32},{32,48},{48,64},{64,80},{80,96},{96,112},{112,0},{1... | collective-permute-start | bytes 393224 | tf_op jit(solution)/shard_map/ppermute | solution.py:25
  19.8 17.8 %collective-permute-start.6 = (bf16[4,128,256]{2,1,0:T(8,128)(2,1)S(1)}, bf16[4,128,256]{2,1,0:T(8,128)(2,1)S(1)}, u32[]{:S(2)}, u32[]{:S(2)}) collective-permute-start(bf16[4,128,256]{2,1,0:T(8,128)(2,1)S(1)} %constant_dynamic-update-slice_fusion.2.rest_4_), channel_id=1, source_target_pairs={{0,128},{128,0},{1,129},{129,1},{2,130},{130,2},{3,131},{131,3},{4... | collective-permute-start | bytes 786440 | tf_op jit(solution)/shard_map/ppermute | solution.py:29
  22.7 16.3 %collective-permute-start.9 = (bf16[4,128,256]{2,1,0:T(8,128)(2,1)S(1)}, bf16[4,128,256]{2,1,0:T(8,128)(2,1)S(1)}, u32[]{:S(2)}, u32[]{:S(2)}) collective-permute-start(bf16[4,128,256]{2,1,0:T(8,128)(2,1)S(1)} %constant_dynamic-update-slice_fusion.4.rest_6_), channel_id=1, source_target_pairs={{0,128},{128,0},{1,129},{129,1},{2,130},{130,2},{3,131},{131,3},{4... | collective-permute-start | bytes 786440 | tf_op jit(solution)/shard_map/ppermute | solution.py:29
  25.1 12.5 %collective-permute-start = (bf16[2,128,256]{2,1,0:T(8,128)(2,1)}, bf16[2,128,256]{2,1,0:T(8,128)(2,1)S(1)}, u32[]{:S(2)}, u32[]{:S(2)}) collective-permute-start(bf16[2,128,256]{2,1,0:T(8,128)(2,1)} %bitcast.90), channel_id=1, source_target_pairs={{0,128},{128,0},{1,129},{129,1},{2,130},{130,2},{3,131},{131,3},{4... | collective-permute-start | bytes 393224 | tf_op jit(solution)/shard_map/ppermute | solution.py:29
  28.8 10.2 %collective-permute-start.11 = (bf16[2,128,256]{2,1,0:T(8,128)(2,1)S(1)}, bf16[2,128,256]{2,1,0:T(8,128)(2,1)S(1)}, u32[]{:S(2)}, u32[]{:S(2)}) collective-permute-start(bf16[2,128,256]{2,1,0:T(8,128)(2,1)S(1)} %collective-permute-done.10.rest_8_), channel_id=1, source_target_pairs={{0,128},{128,0},{1,129},{129,1},{2,130},{130,2},{3,131},{131,3},{4... | collective-permute-start | bytes 393224 | tf_op jit(solution)/shard_map/ppermute | solution.py:29
  48.8 7.8 %collective-permute-start.12 = (bf16[16,128,256]{2,1,0:T(8,128)(2,1)}, bf16[16,128,256]{2,1,0:T(8,128)(2,1)S(1)}, u32[]{:S(2)}, u32[]{:S(2)}) collective-permute-start(bf16[16,128,256]{2,1,0:T(8,128)(2,1)} %get-tuple-element.28), channel_id=1, source_target_pairs={{0,1},{1,0},{2,3},{3,2},{4,5},{5,4},{6,7},{7,6},{8,9},{9,8},{10,11... | collective-permute-start | bytes 3145736 | tf_op jit(solution)/shard_map/ppermute | solution.py:29
  57.3 10.2 %collective-permute-start.13 = (bf16[2,128,256]{2,1,0:T(8,128)(2,1)S(1)}, bf16[2,128,256]{2,1,0:T(8,128)(2,1)S(1)}, u32[]{:S(2)}, u32[]{:S(2)}) collective-permute-start(bf16[2,128,256]{2,1,0:T(8,128)(2,1)S(1)} %get-tuple-element.30), channel_id=1, source_target_pairs={{0,2},{2,4},{4,6},{6,0},{8,10},{10,12},{12,14},{14,8},{1,3},{3,5},... | collective-permute-start | bytes 393224 | tf_op jit(solution)/shard_map/ppermute | solution.py:37
  57.4 10.2 %collective-permute-start.14 = (bf16[2,128,256]{2,1,0:T(8,128)(2,1)S(1)}, bf16[2,128,256]{2,1,0:T(8,128)(2,1)S(1)}, u32[]{:S(2)}, u32[]{:S(2)}) collective-permute-start(bf16[2,128,256]{2,1,0:T(8,128)(2,1)S(1)} %get-tuple-element.31), channel_id=1, source_target_pairs={{0,4},{2,6},{4,0},{6,2},{8,12},{10,14},{12,8},{14,10},{1,5},{3,7},... | collective-permute-start | bytes 393224 | tf_op jit(solution)/shard_map/ppermute | solution.py:37
  60.2 8.4 %collective-permute-start.15 = (bf16[2,128,256]{2,1,0:T(8,128)(2,1)S(1)}, bf16[2,128,256]{2,1,0:T(8,128)(2,1)S(1)}, u32[]{:S(2)}, u32[]{:S(2)}) collective-permute-start(bf16[2,128,256]{2,1,0:T(8,128)(2,1)S(1)} %get-tuple-element.32), channel_id=1, source_target_pairs={{0,6},{2,0},{4,2},{6,4},{8,14},{10,8},{12,10},{14,12},{1,7},{3,1},... | collective-permute-start | bytes 393224 | tf_op jit(solution)/shard_map/ppermute | solution.py:37
  61.4 7.2 %collective-permute-start.16 = (bf16[2,128,256]{2,1,0:T(8,128)(2,1)S(1)}, bf16[2,128,256]{2,1,0:T(8,128)(2,1)S(1)}, u32[]{:S(2)}, u32[]{:S(2)}) collective-permute-start(bf16[2,128,256]{2,1,0:T(8,128)(2,1)S(1)} %get-tuple-element.33), channel_id=1, source_target_pairs={{0,8},{2,10},{4,12},{6,14},{8,0},{10,2},{12,4},{14,6},{1,9},{3,11}... | collective-permute-start | bytes 393224 | tf_op jit(solution)/shard_map/ppermute | solution.py:37
  62.5 9.2 %collective-permute-start.17 = (bf16[2,128,256]{2,1,0:T(8,128)(2,1)S(1)}, bf16[2,128,256]{2,1,0:T(8,128)(2,1)S(1)}, u32[]{:S(2)}, u32[]{:S(2)}) collective-permute-start(bf16[2,128,256]{2,1,0:T(8,128)(2,1)S(1)} %get-tuple-element.34), channel_id=1, source_target_pairs={{0,10},{2,12},{4,14},{6,8},{8,2},{10,4},{12,6},{14,0},{1,11},{3,13... | collective-permute-start | bytes 393224 | tf_op jit(solution)/shard_map/ppermute | solution.py:37
  67.6 8.8 %collective-permute-start.18 = (bf16[2,128,256]{2,1,0:T(8,128)(2,1)S(1)}, bf16[2,128,256]{2,1,0:T(8,128)(2,1)S(1)}, u32[]{:S(2)}, u32[]{:S(2)}) collective-permute-start(bf16[2,128,256]{2,1,0:T(8,128)(2,1)S(1)} %get-tuple-element.35), channel_id=1, source_target_pairs={{0,12},{2,14},{4,8},{6,10},{8,4},{10,6},{12,0},{14,2},{1,13},{3,15... | collective-permute-start | bytes 393224 | tf_op jit(solution)/shard_map/ppermute | solution.py:37
  67.6 8.9 %collective-permute-start.19 = (bf16[2,128,256]{2,1,0:T(8,128)(2,1)S(1)}, bf16[2,128,256]{2,1,0:T(8,128)(2,1)S(1)}, u32[]{:S(2)}, u32[]{:S(2)}) collective-permute-start(bf16[2,128,256]{2,1,0:T(8,128)(2,1)S(1)} %get-tuple-element.36), channel_id=1, source_target_pairs={{0,14},{2,8},{4,10},{6,12},{8,6},{10,0},{12,2},{14,4},{1,15},{3,9}... | collective-permute-start | bytes 393224 | tf_op jit(solution)/shard_map/ppermute | solution.py:37
  77.4 8.2 %collective-permute-start.26 = (bf16[2,256,128]{2,1,0:T(8,128)(2,1)S(1)}, bf16[2,256,128]{2,1,0:T(8,128)(2,1)S(1)}, u32[]{:S(2)}, u32[]{:S(2)}) collective-permute-start(bf16[2,256,128]{2,1,0:T(8,128)(2,1)S(1)} %get-tuple-element.38.rest_0_), channel_id=1, source_target_pairs={{0,14},{2,8},{4,10},{6,12},{8,6},{10,0},{12,2},{14,4},{1,15},{3,9}... | collective-permute-start | bytes 393224 | tf_op jit(solution)/shard_map/ppermute | solution.py:37
  78.0 9.1 %collective-permute-start.25 = (bf16[2,256,128]{2,1,0:T(8,128)(2,1)S(1)}, bf16[2,256,128]{2,1,0:T(8,128)(2,1)S(1)}, u32[]{:S(2)}, u32[]{:S(2)}) collective-permute-start(bf16[2,256,128]{2,1,0:T(8,128)(2,1)S(1)} %get-tuple-element.38.rest_0_), channel_id=1, source_target_pairs={{0,12},{2,14},{4,8},{6,10},{8,4},{10,6},{12,0},{14,2},{1,13},{3,15... | collective-permute-start | bytes 393224 | tf_op jit(solution)/shard_map/ppermute | solution.py:37
  80.2 10.1 %collective-permute-start.24 = (bf16[2,256,128]{2,1,0:T(8,128)(2,1)S(1)}, bf16[2,256,128]{2,1,0:T(8,128)(2,1)S(1)}, u32[]{:S(2)}, u32[]{:S(2)}) collective-permute-start(bf16[2,256,128]{2,1,0:T(8,128)(2,1)S(1)} %get-tuple-element.38.rest_0_), channel_id=1, source_target_pairs={{0,10},{2,12},{4,14},{6,8},{8,2},{10,4},{12,6},{14,0},{1,11},{3,13... | collective-permute-start | bytes 393224 | tf_op jit(solution)/shard_map/ppermute | solution.py:37
  81.1 11.5 %collective-permute-start.23 = (bf16[2,256,128]{2,1,0:T(8,128)(2,1)S(1)}, bf16[2,256,128]{2,1,0:T(8,128)(2,1)S(1)}, u32[]{:S(2)}, u32[]{:S(2)}) collective-permute-start(bf16[2,256,128]{2,1,0:T(8,128)(2,1)S(1)} %get-tuple-element.38.rest_0_), channel_id=1, source_target_pairs={{0,8},{2,10},{4,12},{6,14},{8,0},{10,2},{12,4},{14,6},{1,9},{3,11}... | collective-permute-start | bytes 393224 | tf_op jit(solution)/shard_map/ppermute | solution.py:37
  82.4 10.2 %collective-permute-start.22 = (bf16[2,256,128]{2,1,0:T(8,128)(2,1)S(1)}, bf16[2,256,128]{2,1,0:T(8,128)(2,1)S(1)}, u32[]{:S(2)}, u32[]{:S(2)}) collective-permute-start(bf16[2,256,128]{2,1,0:T(8,128)(2,1)S(1)} %get-tuple-element.38.rest_0_), channel_id=1, source_target_pairs={{0,6},{2,0},{4,2},{6,4},{8,14},{10,8},{12,10},{14,12},{1,7},{3,1},... | collective-permute-start | bytes 393224 | tf_op jit(solution)/shard_map/ppermute | solution.py:37
  85.5 7.6 %collective-permute-start.21 = (bf16[2,256,128]{2,1,0:T(8,128)(2,1)S(1)}, bf16[2,256,128]{2,1,0:T(8,128)(2,1)S(1)}, u32[]{:S(2)}, u32[]{:S(2)}) collective-permute-start(bf16[2,256,128]{2,1,0:T(8,128)(2,1)S(1)} %get-tuple-element.38.rest_0_), channel_id=1, source_target_pairs={{0,4},{2,6},{4,0},{6,2},{8,12},{10,14},{12,8},{14,10},{1,5},{3,7},... | collective-permute-start | bytes 393224 | tf_op jit(solution)/shard_map/ppermute | solution.py:37
  87.2 8.2 %collective-permute-start.20 = (bf16[2,256,128]{2,1,0:T(8,128)(2,1)S(1)}, bf16[2,256,128]{2,1,0:T(8,128)(2,1)S(1)}, u32[]{:S(2)}, u32[]{:S(2)}) collective-permute-start(bf16[2,256,128]{2,1,0:T(8,128)(2,1)S(1)} %get-tuple-element.38.rest_0_), channel_id=1, source_target_pairs={{0,2},{2,4},{4,6},{6,0},{8,10},{10,12},{12,14},{14,8},{1,3},{3,5},... | collective-permute-start | bytes 393224 | tf_op jit(solution)/shard_map/ppermute | solution.py:37
  110.4 8.0 %collective-permute-start.35 = (bf16[1,2,256,128]{3,2,1,0:T(8,128)(2,1)S(1)}, bf16[1,2,256,128]{3,2,1,0:T(8,128)(2,1)S(1)}, u32[]{:S(2)}, u32[]{:S(2)}) collective-permute-start(bf16[1,2,256,128]{3,2,1,0:T(8,128)(2,1)S(1)} %get-tuple-element.42), channel_id=1, source_target_pairs={{0,128},{128,0},{1,129},{129,1},{2,130},{130,2},{3,131},{131,3},{4... | collective-permute-start | bytes 393224 | tf_op jit(solution)/shard_map/ppermute | solution.py:29
  110.7 13.2 %collective-permute-start.38 = (bf16[2,2,256,128]{3,2,1,0:T(8,128)(2,1)S(1)}, bf16[2,2,256,128]{3,2,1,0:T(8,128)(2,1)S(1)}, u32[]{:S(2)}, u32[]{:S(2)}) collective-permute-start(bf16[2,2,256,128]{3,2,1,0:T(8,128)(2,1)S(1)} %get-tuple-element.47), channel_id=1, source_target_pairs={{0,128},{128,0},{1,129},{129,1},{2,130},{130,2},{3,131},{131,3},{4... | collective-permute-start | bytes 786440 | tf_op jit(solution)/shard_map/ppermute | solution.py:29
  118.4 6.3 %collective-permute-start.40 = (bf16[2,256,128]{2,1,0:T(8,128)(2,1)S(1)}, bf16[2,256,128]{2,1,0:T(8,128)(2,1)S(1)}, u32[]{:S(2)}, u32[]{:S(2)}) collective-permute-start(bf16[2,256,128]{2,1,0:T(8,128)(2,1)S(1)} %fusion.5), channel_id=1, source_target_pairs={{0,16},{16,32},{32,48},{48,64},{64,80},{80,96},{96,112},{112,0},{1... | collective-permute-start | bytes 393224 | tf_op jit(solution)/shard_map/ppermute | solution.py:25
  118.5 10.7 %collective-permute-start.36 = (bf16[2,2,256,128]{3,2,1,0:T(8,128)(2,1)S(1)}, bf16[2,2,256,128]{3,2,1,0:T(8,128)(2,1)S(1)}, u32[]{:S(2)}, u32[]{:S(2)}) collective-permute-start(bf16[2,2,256,128]{3,2,1,0:T(8,128)(2,1)S(1)} %get-tuple-element.43), channel_id=1, source_target_pairs={{0,128},{128,0},{1,129},{129,1},{2,130},{130,2},{3,131},{131,3},{4... | collective-permute-start | bytes 786440 | tf_op jit(solution)/shard_map/ppermute | solution.py:29
  124.7 6.3 %collective-permute-start.41 = (bf16[2,256,128]{2,1,0:T(8,128)(2,1)S(1)}, bf16[2,256,128]{2,1,0:T(8,128)(2,1)S(1)}, u32[]{:S(2)}, u32[]{:S(2)}) collective-permute-start(bf16[2,256,128]{2,1,0:T(8,128)(2,1)S(1)} %fusion.2), channel_id=1, source_target_pairs={{0,16},{16,32},{32,48},{48,64},{64,80},{80,96},{96,112},{112,0},{1... | collective-permute-start | bytes 393224 | tf_op jit(solution)/shard_map/ppermute | solution.py:25
  126.2 8.7 %collective-permute-start.39 = (bf16[2,2,256,128]{3,2,1,0:T(8,128)(2,1)S(1)}, bf16[2,2,256,128]{3,2,1,0:T(8,128)(2,1)S(1)}, u32[]{:S(2)}, u32[]{:S(2)}) collective-permute-start(bf16[2,2,256,128]{3,2,1,0:T(8,128)(2,1)S(1)} %get-tuple-element.48), channel_id=1, source_target_pairs={{0,128},{128,0},{1,129},{129,1},{2,130},{130,2},{3,131},{131,3},{4... | collective-permute-start | bytes 786440 | tf_op jit(solution)/shard_map/ppermute | solution.py:29
  131.1 6.4 %collective-permute-start.42 = (bf16[2,256,128]{2,1,0:T(8,128)(2,1)S(1)}, bf16[2,256,128]{2,1,0:T(8,128)(2,1)S(1)}, u32[]{:S(2)}, u32[]{:S(2)}) collective-permute-start(bf16[2,256,128]{2,1,0:T(8,128)(2,1)S(1)} %get-tuple-element.55), channel_id=1, source_target_pairs={{0,16},{16,32},{32,48},{48,64},{64,80},{80,96},{96,112},{112,0},{1... | collective-permute-start | bytes 393224 | tf_op jit(solution)/shard_map/ppermute | solution.py:25
  133.1 6.6 %collective-permute-start.37 = (bf16[1,2,256,128]{3,2,1,0:T(8,128)(2,1)S(1)}, bf16[1,2,256,128]{3,2,1,0:T(8,128)(2,1)S(1)}, u32[]{:S(2)}, u32[]{:S(2)}) collective-permute-start(bf16[1,2,256,128]{3,2,1,0:T(8,128)(2,1)S(1)} %get-tuple-element.44), channel_id=1, source_target_pairs={{0,128},{128,0},{1,129},{129,1},{2,130},{130,2},{3,131},{131,3},{4... | collective-permute-start | bytes 393224 | tf_op jit(solution)/shard_map/ppermute | solution.py:29
  (30 other events, 252.9 us)
where the time goes:
time: 146 us
  waiting for transfers between devices  57.5 us (39%)
  starting transfers between devices  53.2 us (36%)
  Pallas kernels  30.4 us (21%)
  local copies, waits for them, and re-layouts  3.42 us (2%)
    ppermute x19, waiting for transfers between devices, swap(): return lax.ppermute(value, axis, [(0, 1), (1, 0)])  21.2 us
    ppermute x14, waiting for transfers between devices, plane_send(): return lax.ppermute(value, ('yl', 'x'), pairs)  19.1 us
    ppermute x14, starting transfers between devices, shift(): lax.ppermute(value, axis, [(i, (i + step) % size) for i in range(size)])  18.6 us
    ppermute x14, starting transfers between devices, plane_send(): return lax.ppermute(value, ('yl', 'x'), pairs)  17.4 us
    ppermute x19, starting transfers between devices, swap(): return lax.ppermute(value, axis, [(0, 1), (1, 0)])  17.2 us
    ppermute x14, waiting for transfers between devices, shift(): lax.ppermute(value, axis, [(i, (i + step) % size) for i in range(size)])  17.2 us
    pallas_call x2, Pallas kernels, forward(): pl.pallas_call(functools.partial(forward_body, n=n, first=first), out_sha...  14.8 us
    pallas_call x1, Pallas kernels, backward(): pl.pallas_call(functools.partial(backward_body, n=n), out_shape=[jax.Shap...  13.1 us
  transfers between devices with their start and end apart: 47, of which 27 were waited for; matrix products, arithmetic and copies ran while one was open for 1% of the time, Pallas kernels for 4%

commit v1 on v0

--- a/solution.py
+++ b/solution.py
@@ -37,7 +37,7 @@
     return lax.ppermute(value, ("yl", "x"), pairs)
 
 
-PLANE = [(dy, dx) for dy in range(NY) for dx in range(NX)]
+PLANE = [(0, 0), (0, 1), (1, 1), (0, 3), (1, 3), (0, 2), (1, 0), (1, 2)]
 
 
 def tile_row(u, core):

time: 146 us -> 150 us (1.027)
  starting transfers between devices: 53.2 us -> 77.2 us
  waiting for transfers between devices: 57.5 us -> 43.8 us
  Pallas kernels: 30.4 us -> 24.3 us
    ppermute x14, starting transfers between devices: 17.4 us -> 31.3 us  [plane_send(): return lax.ppermute(value, ('yl', 'x'), pairs)]
    ppermute x14, waiting for transfers between devices: 19.1 us -> 7.8 us  [plane_send(): return lax.ppermute(value, ('yl', 'x'), pairs)]
    ppermute x19, starting transfers between devices: 17.2 us -> 25.1 us  [swap(): return lax.ppermute(value, axis, [(0, 1), (1, 0)])]
    ppermute x19, waiting for transfers between devices: 21.2 us -> 16 us  [swap(): return lax.ppermute(value, axis, [(0, 1), (1, 0)])]
    pallas_call x1, Pallas kernels: 13.1 us -> 9.26 us  [backward(): pl.pallas_call(functools.partial(backward_body, n=n), out_shape=[jax.Shap...]
    ppermute x14, waiting for transfers between devices: 17.2 us -> 20 us  [shift(): lax.ppermute(value, axis, [(i, (i + step) % size) for i in range(size)])]
    pallas_call x2, Pallas kernels: 14.8 us -> 12.6 us  [forward(): pl.pallas_call(functools.partial(forward_body, n=n, first=first), out_sha...]
    ppermute x14, starting transfers between devices: 18.6 us -> 20.8 us  [shift(): lax.ppermute(value, axis, [(i, (i + step) % size) for i in range(size)])]
  transfers between devices with their start and end apart: 47 -> 47, of which waited for: 27 -> 22; matrix products, arithmetic and copies ran while one was open for 1% -> 1% of each run, Pallas kernels for 4% -> 3%
where the time goes in v1:
time: 150 us
  starting transfers between devices  77.2 us (51%)
  waiting for transfers between devices  43.8 us (29%)
  Pallas kernels  24.3 us (16%)
  local copies, waits for them, and re-layouts  3.42 us (2%)
    ppermute x14, starting transfers between devices, plane_send(): return lax.ppermute(value, ('yl', 'x'), pairs)  31.3 us
    ppermute x19, starting transfers between devices, swap(): return lax.ppermute(value, axis, [(0, 1), (1, 0)])  25.1 us
    ppermute x14, starting transfers between devices, shift(): lax.ppermute(value, axis, [(i, (i + step) % size) for i in range(size)])  20.8 us
    ppermute x14, waiting for transfers between devices, shift(): lax.ppermute(value, axis, [(i, (i + step) % size) for i in range(size)])  20 us
    ppermute x19, waiting for transfers between devices, swap(): return lax.ppermute(value, axis, [(0, 1), (1, 0)])  16 us
    pallas_call x2, Pallas kernels, forward(): pl.pallas_call(functools.partial(forward_body, n=n, first=first), out_sha...  12.6 us
    pallas_call x1, Pallas kernels, backward(): pl.pallas_call(functools.partial(backward_body, n=n), out_shape=[jax.Shap...  9.26 us
    ppermute x14, waiting for transfers between devices, plane_send(): return lax.ppermute(value, ('yl', 'x'), pairs)  7.8 us
  transfers between devices with their start and end apart: 47, of which 22 were waited for; matrix products, arithmetic and copies ran while one was open for 1% of the time, Pallas kernels for 3%

profile of v1, /device:TPU:8, one launch (start us, length us, event | category | flops | bytes accessed | tf_op | source)
XLA Modules:
  0.0 150.0 jit_solution(13076459587400595084)
XLA Ops:
  0.6 2.0 %collective-permute-start.1 = (bf16[2,128,256]{2,1,0:T(8,128)(2,1)}, bf16[2,128,256]{2,1,0:T(8,128)(2,1)S(1)}, u32[]{:S(2)}, u32[]{:S(2)}) collective-permute-start(bf16[2,128,256]{2,1,0:T(8,128)(2,1)} %bitcast.88), channel_id=1, source_target_pairs={{0,16},{16,32},{32,48},{48,64},{64,80},{80,96},{96,112},{112,0},{1... | collective-permute-start | bytes 393224 | tf_op jit(solution)/shard_map/ppermute | solution.py:25
  2.6 4.0 %collective-permute-start.2 = (bf16[2,128,256]{2,1,0:T(8,128)(2,1)}, bf16[2,128,256]{2,1,0:T(8,128)(2,1)S(1)}, u32[]{:S(2)}, u32[]{:S(2)}) collective-permute-start(bf16[2,128,256]{2,1,0:T(8,128)(2,1)} %bitcast.89), channel_id=1, source_target_pairs={{0,112},{16,0},{32,16},{48,32},{64,48},{80,64},{96,80},{112,96},{1... | collective-permute-start | bytes 393224 | tf_op jit(solution)/shard_map/ppermute | solution.py:25
  6.7 3.6 %collective-permute-done.1 = bf16[2,128,256]{2,1,0:T(8,128)(2,1)S(1)} collective-permute-done((bf16[2,128,256]{2,1,0:T(8,128)(2,1)}, bf16[2,128,256]{2,1,0:T(8,128)(2,1)S(1)}, u32[]{:S(2)}, u32[]{:S(2)}) %collective-permute-start.1) | collective-permute-done | bytes 131104 | tf_op jit(solution)/shard_map/ppermute | solution.py:25
  10.3 3.3 %collective-permute-start.5 = (bf16[2,128,256]{2,1,0:T(8,128)(2,1)S(1)}, bf16[2,128,256]{2,1,0:T(8,128)(2,1)S(1)}, u32[]{:S(2)}, u32[]{:S(2)}) collective-permute-start(bf16[2,128,256]{2,1,0:T(8,128)(2,1)S(1)} %collective-permute-done.2), channel_id=1, source_target_pairs={{0,112},{16,0},{32,16},{48,32},{64,48},{80,64},{96,80},{112,96},{1... | collective-permute-start | bytes 393224 | tf_op jit(solution)/shard_map/ppermute | solution.py:25
  13.7 2.4 %collective-permute-start.3 = (bf16[4,128,256]{2,1,0:T(8,128)(2,1)S(1)}, bf16[4,128,256]{2,1,0:T(8,128)(2,1)S(1)}, u32[]{:S(2)}, u32[]{:S(2)}) collective-permute-start(bf16[4,128,256]{2,1,0:T(8,128)(2,1)S(1)} %constant_dynamic-update-slice_fusion.rest_2_), channel_id=1, source_target_pairs={{0,128},{128,0},{1,129},{129,1},{2,130},{130,2},{3,131},{131,3},{4... | collective-permute-start | bytes 786440 | tf_op jit(solution)/shard_map/ppermute | solution.py:29
  16.5 3.3 %collective-permute-start.8 = (bf16[2,128,256]{2,1,0:T(8,128)(2,1)S(1)}, bf16[2,128,256]{2,1,0:T(8,128)(2,1)S(1)}, u32[]{:S(2)}, u32[]{:S(2)}) collective-permute-start(bf16[2,128,256]{2,1,0:T(8,128)(2,1)S(1)} %collective-permute-done.5), channel_id=1, source_target_pairs={{0,112},{16,0},{32,16},{48,32},{64,48},{80,64},{96,80},{112,96},{1... | collective-permute-start | bytes 393224 | tf_op jit(solution)/shard_map/ppermute | solution.py:25
  19.8 2.4 %collective-permute-start.6 = (bf16[4,128,256]{2,1,0:T(8,128)(2,1)S(1)}, bf16[4,128,256]{2,1,0:T(8,128)(2,1)S(1)}, u32[]{:S(2)}, u32[]{:S(2)}) collective-permute-start(bf16[4,128,256]{2,1,0:T(8,128)(2,1)S(1)} %constant_dynamic-update-slice_fusion.2.rest_4_), channel_id=1, source_target_pairs={{0,128},{128,0},{1,129},{129,1},{2,130},{130,2},{3,131},{131,3},{4... | collective-permute-start | bytes 786440 | tf_op jit(solution)/shard_map/ppermute | solution.py:29
  22.7 2.4 %collective-permute-start.9 = (bf16[4,128,256]{2,1,0:T(8,128)(2,1)S(1)}, bf16[4,128,256]{2,1,0:T(8,128)(2,1)S(1)}, u32[]{:S(2)}, u32[]{:S(2)}) collective-permute-start(bf16[4,128,256]{2,1,0:T(8,128)(2,1)S(1)} %constant_dynamic-update-slice_fusion.4.rest_6_), channel_id=1, source_target_pairs={{0,128},{128,0},{1,129},{129,1},{2,130},{130,2},{3,131},{131,3},{4... | collective-permute-start | bytes 786440 | tf_op jit(solution)/shard_map/ppermute | solution.py:29
  26.3 2.5 %collective-permute-done.10.rest_8_ = bf16[2,128,256]{2,1,0:T(8,128)(2,1)S(1)} collective-permute-done((bf16[2,128,256]{2,1,0:T(8,128)(2,1)S(1)}, bf16[2,128,256]{2,1,0:T(8,128)(2,1)S(1)}, u32[]{:S(2)}, u32[]{:S(2)}) %collective-permute-start.10) | collective-permute-done | bytes 131104 | tf_op jit(solution)/shard_map/ppermute | solution.py:25
  28.8 2.3 %collective-permute-start.11 = (bf16[2,128,256]{2,1,0:T(8,128)(2,1)S(1)}, bf16[2,128,256]{2,1,0:T(8,128)(2,1)S(1)}, u32[]{:S(2)}, u32[]{:S(2)}) collective-permute-start(bf16[2,128,256]{2,1,0:T(8,128)(2,1)S(1)} %collective-permute-done.10.rest_8_), channel_id=1, source_target_pairs={{0,128},{128,0},{1,129},{129,1},{2,130},{130,2},{3,131},{131,3},{4... | collective-permute-start | bytes 393224 | tf_op jit(solution)/shard_map/ppermute | solution.py:29
  32.1 5.6 %collective-permute-done.rest_1_ = bf16[2,128,256]{2,1,0:T(8,128)(2,1)S(1)} collective-permute-done((bf16[2,128,256]{2,1,0:T(8,128)(2,1)}, bf16[2,128,256]{2,1,0:T(8,128)(2,1)S(1)}, u32[]{:S(2)}, u32[]{:S(2)}) %collective-permute-start) | collective-permute-done | bytes 131104 | tf_op jit(solution)/shard_map/ppermute | solution.py:29
  39.8 7.7 %forward.2 = (bf16[16,128,256]{2,1,0:T(8,128)(2,1)}, bf16[32,128,256]{2,1,0:T(8,128)(2,1)}) custom-call(s32[465]{0:T(512)} %concatenate.12.meta_ref, bf16[32,12,128,128]{3,2,1,0:T(8,128)(2,1)} %bitcast.84, bf16[2,128,256]{2,1,0:T(8,128)(2,1)} %bitcast.91, bf16[2,128,256]{2,1,0:T(8,128)(2,1)} %copy-done.13, bf16[4,128,256]{2,1,0:T(8,128)(2,1)} %copy-done.5, ...), custom_call_target="tpu_custom_call" | custom-call | flops 4000000000 | bytes 9437184 | tf_op jit(solution)/shard_map/forward/pallas_call | solution.py:131
  49.4 4.9 %forward.3.mine_ref = f32[16,128,256]{2,1,0:T(8,128)S(1)} custom-call(s32[465]{0:T(512)S(1)} %copy-done.3, bf16[32,12,128,128]{3,2,1,0:T(8,128)(2,1)} %bitcast.85, bf16[32,128,256]{2,1,0:T(8,128)(2,1)S(1)} %copy-done), custom_call_target="tpu_custom_call" | custom-call | flops 4000000000 | bytes 9437184 | tf_op jit(solution)/shard_map/forward/pallas_call | solution.py:131
  55.1 3.8 %collective-permute-start.13 = (bf16[2,128,256]{2,1,0:T(8,128)(2,1)S(1)}, bf16[2,128,256]{2,1,0:T(8,128)(2,1)S(1)}, u32[]{:S(2)}, u32[]{:S(2)}) collective-permute-start(bf16[2,128,256]{2,1,0:T(8,128)(2,1)S(1)} %get-tuple-element.30), channel_id=1, source_target_pairs={{0,2},{2,4},{4,6},{6,0},{8,10},{10,12},{12,14},{14,8},{1,3},{3,5},... | collective-permute-start | bytes 393224 | tf_op jit(solution)/shard_map/ppermute | solution.py:37
  67.2 2.9 %collective-permute-start.19 = (bf16[2,128,256]{2,1,0:T(8,128)(2,1)S(1)}, bf16[2,128,256]{2,1,0:T(8,128)(2,1)S(1)}, u32[]{:S(2)}, u32[]{:S(2)}) collective-permute-start(bf16[2,128,256]{2,1,0:T(8,128)(2,1)S(1)} %get-tuple-element.36), channel_id=1, source_target_pairs={{0,12},{2,14},{4,8},{6,10},{8,4},{10,6},{12,0},{14,2},{1,13},{3,15... | collective-permute-start | bytes 393224 | tf_op jit(solution)/shard_map/ppermute | solution.py:37
  70.7 4.1 %collective-permute-done.18.refs_6_ = bf16[2,128,256]{2,1,0:T(8,128)(2,1)S(1)} collective-permute-done((bf16[2,128,256]{2,1,0:T(8,128)(2,1)S(1)}, bf16[2,128,256]{2,1,0:T(8,128)(2,1)S(1)}, u32[]{:S(2)}, u32[]{:S(2)}) %collective-permute-start.18) | collective-permute-done | bytes 131104 | tf_op jit(solution)/shard_map/ppermute | solution.py:37
  75.8 2.7 %collective-permute-start.26 = (bf16[2,256,128]{2,1,0:T(8,128)(2,1)S(1)}, bf16[2,256,128]{2,1,0:T(8,128)(2,1)S(1)}, u32[]{:S(2)}, u32[]{:S(2)}) collective-permute-start(bf16[2,256,128]{2,1,0:T(8,128)(2,1)S(1)} %get-tuple-element.38.rest_0_), channel_id=1, source_target_pairs={{0,12},{2,14},{4,8},{6,10},{8,4},{10,6},{12,0},{14,2},{1,13},{3,15... | collective-permute-start | bytes 393224 | tf_op jit(solution)/shard_map/ppermute | solution.py:37
  80.8 3.2 %collective-permute-start.23 = (bf16[2,256,128]{2,1,0:T(8,128)(2,1)S(1)}, bf16[2,256,128]{2,1,0:T(8,128)(2,1)S(1)}, u32[]{:S(2)}, u32[]{:S(2)}) collective-permute-start(bf16[2,256,128]{2,1,0:T(8,128)(2,1)S(1)} %get-tuple-element.38.rest_0_), channel_id=1, source_target_pairs={{0,14},{2,8},{4,10},{6,12},{8,6},{10,0},{12,2},{14,4},{1,15},{3,9}... | collective-permute-start | bytes 393224 | tf_op jit(solution)/shard_map/ppermute | solution.py:37
  84.2 3.0 %collective-permute-start.21 = (bf16[2,256,128]{2,1,0:T(8,128)(2,1)S(1)}, bf16[2,256,128]{2,1,0:T(8,128)(2,1)S(1)}, u32[]{:S(2)}, u32[]{:S(2)}) collective-permute-start(bf16[2,256,128]{2,1,0:T(8,128)(2,1)S(1)} %get-tuple-element.38.rest_0_), channel_id=1, source_target_pairs={{0,10},{2,12},{4,14},{6,8},{8,2},{10,4},{12,6},{14,0},{1,11},{3,13... | collective-permute-start | bytes 393224 | tf_op jit(solution)/shard_map/ppermute | solution.py:37
  87.1 6.5 %collective-permute-start.20 = (bf16[2,256,128]{2,1,0:T(8,128)(2,1)S(1)}, bf16[2,256,128]{2,1,0:T(8,128)(2,1)S(1)}, u32[]{:S(2)}, u32[]{:S(2)}) collective-permute-start(bf16[2,256,128]{2,1,0:T(8,128)(2,1)S(1)} %get-tuple-element.38.rest_0_), channel_id=1, source_target_pairs={{0,2},{2,4},{4,6},{6,0},{8,10},{10,12},{12,14},{14,8},{1,3},{3,5},... | collective-permute-start | bytes 393224 | tf_op jit(solution)/shard_map/ppermute | solution.py:37
  98.0 9.3 %backward.1 = (bf16[1,2,256,128]{3,2,1,0:T(8,128)(2,1)S(1)}, bf16[2,2,256,128]{3,2,1,0:T(8,128)(2,1)S(1)}, bf16[2,2,256,128]{3,2,1,0:T(8,128)(2,1)S(1)}, bf16[2,...) custom-call(s32[465]{0:T(512)S(1)} %copy-done.3, ...), custom_call_target="tpu_custom_call" | custom-call | flops 8000000000 | bytes 18874368 | tf_op jit(solution)/shard_map/backward/pallas_call | solution.py:188
  107.3 6.7 %collective-permute-start.35 = (bf16[1,2,256,128]{3,2,1,0:T(8,128)(2,1)S(1)}, bf16[1,2,256,128]{3,2,1,0:T(8,128)(2,1)S(1)}, u32[]{:S(2)}, u32[]{:S(2)}) collective-permute-start(bf16[1,2,256,128]{3,2,1,0:T(8,128)(2,1)S(1)} %get-tuple-element.42), channel_id=1, source_target_pairs={{0,128},{128,0},{1,129},{129,1},{2,130},{130,2},{3,131},{131,3},{4... | collective-permute-start | bytes 393224 | tf_op jit(solution)/shard_map/ppermute | solution.py:29
  114.1 2.8 %collective-permute-done.35 = bf16[1,2,256,128]{3,2,1,0:T(8,128)(2,1)S(1)} collective-permute-done((bf16[1,2,256,128]{3,2,1,0:T(8,128)(2,1)S(1)}, bf16[1,2,256,128]{3,2,1,0:T(8,128)(2,1)S(1)}, u32[]{:S(2)}, u32[]{:S(2)}) %collective-permute-start.35) | collective-permute-done | bytes 131104 | tf_op jit(solution)/shard_map/ppermute | solution.py:29
  118.3 2.4 %collective-permute-start.36 = (bf16[2,2,256,128]{3,2,1,0:T(8,128)(2,1)S(1)}, bf16[2,2,256,128]{3,2,1,0:T(8,128)(2,1)S(1)}, u32[]{:S(2)}, u32[]{:S(2)}) collective-permute-start(bf16[2,2,256,128]{3,2,1,0:T(8,128)(2,1)S(1)} %get-tuple-element.43), channel_id=1, source_target_pairs={{0,128},{128,0},{1,129},{129,1},{2,130},{130,2},{3,131},{131,3},{4... | collective-permute-start | bytes 786440 | tf_op jit(solution)/shard_map/ppermute | solution.py:29
  120.6 3.0 %collective-permute-done.38 = bf16[2,2,256,128]{3,2,1,0:T(8,128)(2,1)S(1)} collective-permute-done((bf16[2,2,256,128]{3,2,1,0:T(8,128)(2,1)S(1)}, bf16[2,2,256,128]{3,2,1,0:T(8,128)(2,1)S(1)}, u32[]{:S(2)}, u32[]{:S(2)}) %collective-permute-start.38) | collective-permute-done | bytes 262176 | tf_op jit(solution)/shard_map/ppermute | solution.py:29
  127.2 2.0 %collective-permute-done.36 = bf16[2,2,256,128]{3,2,1,0:T(8,128)(2,1)S(1)} collective-permute-done((bf16[2,2,256,128]{3,2,1,0:T(8,128)(2,1)S(1)}, bf16[2,2,256,128]{3,2,1,0:T(8,128)(2,1)S(1)}, u32[]{:S(2)}, u32[]{:S(2)}) %collective-permute-start.36) | collective-permute-done | bytes 262176 | tf_op jit(solution)/shard_map/ppermute | solution.py:29
  130.8 2.2 %collective-permute-start.45 = (bf16[2,256,128]{2,1,0:T(8,128)(2,1)S(1)}, bf16[2,256,128]{2,1,0:T(8,128)(2,1)S(1)}, u32[]{:S(2)}, u32[]{:S(2)}) collective-permute-start(bf16[2,256,128]{2,1,0:T(8,128)(2,1)S(1)} %get-tuple-element.54), channel_id=1, source_target_pairs={{0,112},{16,0},{32,16},{48,32},{64,48},{80,64},{96,80},{112,96},{1... | collective-permute-start | bytes 393224 | tf_op jit(solution)/shard_map/ppermute | solution.py:25
  133.1 2.2 %collective-permute-start.37 = (bf16[1,2,256,128]{3,2,1,0:T(8,128)(2,1)S(1)}, bf16[1,2,256,128]{3,2,1,0:T(8,128)(2,1)S(1)}, u32[]{:S(2)}, u32[]{:S(2)}) collective-permute-start(bf16[1,2,256,128]{3,2,1,0:T(8,128)(2,1)S(1)} %get-tuple-element.44), channel_id=1, source_target_pairs={{0,128},{128,0},{1,129},{129,1},{2,130},{130,2},{3,131},{131,3},{4... | collective-permute-start | bytes 393224 | tf_op jit(solution)/shard_map/ppermute | solution.py:29
  136.6 2.7 %collective-permute-done.42 = bf16[2,256,128]{2,1,0:T(8,128)(2,1)S(1)} collective-permute-done((bf16[2,256,128]{2,1,0:T(8,128)(2,1)S(1)}, bf16[2,256,128]{2,1,0:T(8,128)(2,1)S(1)}, u32[]{:S(2)}, u32[]{:S(2)}) %collective-permute-start.42) | collective-permute-done | bytes 131104 | tf_op jit(solution)/shard_map/ppermute | solution.py:25
  139.4 2.4 %collective-permute-start.46 = (bf16[2,256,128]{2,1,0:T(8,128)(2,1)S(1)}, bf16[2,256,128]{2,1,0:T(8,128)(2,1)S(1)}, u32[]{:S(2)}, u32[]{:S(2)}) collective-permute-start(bf16[2,256,128]{2,1,0:T(8,128)(2,1)S(1)} %get-tuple-element.52), channel_id=1, source_target_pairs={{0,112},{16,0},{32,16},{48,32},{64,48},{80,64},{96,80},{112,96},{1... | collective-permute-start | bytes 393224 | tf_op jit(solution)/shard_map/ppermute | solution.py:25
  141.8 2.6 %collective-permute-done.46.rest_1_ = bf16[2,256,128]{2,1,0:T(8,128)(2,1)S(1)} collective-permute-done((bf16[2,256,128]{2,1,0:T(8,128)(2,1)S(1)}, bf16[2,256,128]{2,1,0:T(8,128)(2,1)S(1)}, u32[]{:S(2)}, u32[]{:S(2)}) %collective-permute-start.46) | collective-permute-done | bytes 131104 | tf_op jit(solution)/shard_map/ppermute | solution.py:25
  144.4 4.8 %collective-permute-done.43.rest_0_ = bf16[2,256,128]{2,1,0:T(8,128)(2,1)S(1)} collective-permute-done((bf16[2,256,128]{2,1,0:T(8,128)(2,1)S(1)}, bf16[2,256,128]{2,1,0:T(8,128)(2,1)S(1)}, u32[]{:S(2)}, u32[]{:S(2)}) %collective-permute-start.43) | collective-permute-done | bytes 131104 | tf_op jit(solution)/shard_map/ppermute | solution.py:25
  (113 shorter events, 33.5 us)
Async XLA Ops:
  0.6 9.6 %collective-permute-start.1 = (bf16[2,128,256]{2,1,0:T(8,128)(2,1)}, bf16[2,128,256]{2,1,0:T(8,128)(2,1)S(1)}, u32[]{:S(2)}, u32[]{:S(2)}) collective-permute-start(bf16[2,128,256]{2,1,0:T(8,128)(2,1)} %bitcast.88), channel_id=1, source_target_pairs={{0,16},{16,32},{32,48},{48,64},{64,80},{80,96},{96,112},{112,0},{1... | collective-permute-start | bytes 393224 | tf_op jit(solution)/shard_map/ppermute | solution.py:25
  2.6 7.7 %collective-permute-start.2 = (bf16[2,128,256]{2,1,0:T(8,128)(2,1)}, bf16[2,128,256]{2,1,0:T(8,128)(2,1)S(1)}, u32[]{:S(2)}, u32[]{:S(2)}) collective-permute-start(bf16[2,128,256]{2,1,0:T(8,128)(2,1)} %bitcast.89), channel_id=1, source_target_pairs={{0,112},{16,0},{32,16},{48,32},{64,48},{80,64},{96,80},{112,96},{1... | collective-permute-start | bytes 393224 | tf_op jit(solution)/shard_map/ppermute | solution.py:25
  13.7 24.0 %collective-permute-start.3 = (bf16[4,128,256]{2,1,0:T(8,128)(2,1)S(1)}, bf16[4,128,256]{2,1,0:T(8,128)(2,1)S(1)}, u32[]{:S(2)}, u32[]{:S(2)}) collective-permute-start(bf16[4,128,256]{2,1,0:T(8,128)(2,1)S(1)} %constant_dynamic-update-slice_fusion.rest_2_), channel_id=1, source_target_pairs={{0,128},{128,0},{1,129},{129,1},{2,130},{130,2},{3,131},{131,3},{4... | collective-permute-start | bytes 786440 | tf_op jit(solution)/shard_map/ppermute | solution.py:29
  19.8 17.8 %collective-permute-start.6 = (bf16[4,128,256]{2,1,0:T(8,128)(2,1)S(1)}, bf16[4,128,256]{2,1,0:T(8,128)(2,1)S(1)}, u32[]{:S(2)}, u32[]{:S(2)}) collective-permute-start(bf16[4,128,256]{2,1,0:T(8,128)(2,1)S(1)} %constant_dynamic-update-slice_fusion.2.rest_4_), channel_id=1, source_target_pairs={{0,128},{128,0},{1,129},{129,1},{2,130},{130,2},{3,131},{131,3},{4... | collective-permute-start | bytes 786440 | tf_op jit(solution)/shard_map/ppermute | solution.py:29
  22.7 16.3 %collective-permute-start.9 = (bf16[4,128,256]{2,1,0:T(8,128)(2,1)S(1)}, bf16[4,128,256]{2,1,0:T(8,128)(2,1)S(1)}, u32[]{:S(2)}, u32[]{:S(2)}) collective-permute-start(bf16[4,128,256]{2,1,0:T(8,128)(2,1)S(1)} %constant_dynamic-update-slice_fusion.4.rest_6_), channel_id=1, source_target_pairs={{0,128},{128,0},{1,129},{129,1},{2,130},{130,2},{3,131},{131,3},{4... | collective-permute-start | bytes 786440 | tf_op jit(solution)/shard_map/ppermute | solution.py:29
  25.1 12.5 %collective-permute-start = (bf16[2,128,256]{2,1,0:T(8,128)(2,1)}, bf16[2,128,256]{2,1,0:T(8,128)(2,1)S(1)}, u32[]{:S(2)}, u32[]{:S(2)}) collective-permute-start(bf16[2,128,256]{2,1,0:T(8,128)(2,1)} %bitcast.90), channel_id=1, source_target_pairs={{0,128},{128,0},{1,129},{129,1},{2,130},{130,2},{3,131},{131,3},{4... | collective-permute-start | bytes 393224 | tf_op jit(solution)/shard_map/ppermute | solution.py:29
  28.8 10.2 %collective-permute-start.11 = (bf16[2,128,256]{2,1,0:T(8,128)(2,1)S(1)}, bf16[2,128,256]{2,1,0:T(8,128)(2,1)S(1)}, u32[]{:S(2)}, u32[]{:S(2)}) collective-permute-start(bf16[2,128,256]{2,1,0:T(8,128)(2,1)S(1)} %collective-permute-done.10.rest_8_), channel_id=1, source_target_pairs={{0,128},{128,0},{1,129},{129,1},{2,130},{130,2},{3,131},{131,3},{4... | collective-permute-start | bytes 393224 | tf_op jit(solution)/shard_map/ppermute | solution.py:29
  47.5 6.8 %collective-permute-start.12 = (bf16[16,128,256]{2,1,0:T(8,128)(2,1)}, bf16[16,128,256]{2,1,0:T(8,128)(2,1)S(1)}, u32[]{:S(2)}, u32[]{:S(2)}) collective-permute-start(bf16[16,128,256]{2,1,0:T(8,128)(2,1)} %get-tuple-element.28), channel_id=1, source_target_pairs={{0,1},{1,0},{2,3},{3,2},{4,5},{5,4},{6,7},{7,6},{8,9},{9,8},{10,11... | collective-permute-start | bytes 3145736 | tf_op jit(solution)/shard_map/ppermute | solution.py:29
  55.1 9.5 %collective-permute-start.13 = (bf16[2,128,256]{2,1,0:T(8,128)(2,1)S(1)}, bf16[2,128,256]{2,1,0:T(8,128)(2,1)S(1)}, u32[]{:S(2)}, u32[]{:S(2)}) collective-permute-start(bf16[2,128,256]{2,1,0:T(8,128)(2,1)S(1)} %get-tuple-element.30), channel_id=1, source_target_pairs={{0,2},{2,4},{4,6},{6,0},{8,10},{10,12},{12,14},{14,8},{1,3},{3,5},... | collective-permute-start | bytes 393224 | tf_op jit(solution)/shard_map/ppermute | solution.py:37
  58.9 8.3 %collective-permute-start.14 = (bf16[2,128,256]{2,1,0:T(8,128)(2,1)S(1)}, bf16[2,128,256]{2,1,0:T(8,128)(2,1)S(1)}, u32[]{:S(2)}, u32[]{:S(2)}) collective-permute-start(bf16[2,128,256]{2,1,0:T(8,128)(2,1)S(1)} %get-tuple-element.31), channel_id=1, source_target_pairs={{0,10},{2,12},{4,14},{6,8},{8,2},{10,4},{12,6},{14,0},{1,11},{3,13... | collective-permute-start | bytes 393224 | tf_op jit(solution)/shard_map/ppermute | solution.py:37
  60.2 9.9 %collective-permute-start.15 = (bf16[2,128,256]{2,1,0:T(8,128)(2,1)S(1)}, bf16[2,128,256]{2,1,0:T(8,128)(2,1)S(1)}, u32[]{:S(2)}, u32[]{:S(2)}) collective-permute-start(bf16[2,128,256]{2,1,0:T(8,128)(2,1)S(1)} %get-tuple-element.32), channel_id=1, source_target_pairs={{0,6},{2,0},{4,2},{6,4},{8,14},{10,8},{12,10},{14,12},{1,7},{3,1},... | collective-permute-start | bytes 393224 | tf_op jit(solution)/shard_map/ppermute | solution.py:37
  61.9 8.2 %collective-permute-start.16 = (bf16[2,128,256]{2,1,0:T(8,128)(2,1)S(1)}, bf16[2,128,256]{2,1,0:T(8,128)(2,1)S(1)}, u32[]{:S(2)}, u32[]{:S(2)}) collective-permute-start(bf16[2,128,256]{2,1,0:T(8,128)(2,1)S(1)} %get-tuple-element.33), channel_id=1, source_target_pairs={{0,14},{2,8},{4,10},{6,12},{8,6},{10,0},{12,2},{14,4},{1,15},{3,9}... | collective-permute-start | bytes 393224 | tf_op jit(solution)/shard_map/ppermute | solution.py:37
  63.4 7.3 %collective-permute-start.17 = (bf16[2,128,256]{2,1,0:T(8,128)(2,1)S(1)}, bf16[2,128,256]{2,1,0:T(8,128)(2,1)S(1)}, u32[]{:S(2)}, u32[]{:S(2)}) collective-permute-start(bf16[2,128,256]{2,1,0:T(8,128)(2,1)S(1)} %get-tuple-element.34), channel_id=1, source_target_pairs={{0,4},{2,6},{4,0},{6,2},{8,12},{10,14},{12,8},{14,10},{1,5},{3,7},... | collective-permute-start | bytes 393224 | tf_op jit(solution)/shard_map/ppermute | solution.py:37
  64.6 10.2 %collective-permute-start.18 = (bf16[2,128,256]{2,1,0:T(8,128)(2,1)S(1)}, bf16[2,128,256]{2,1,0:T(8,128)(2,1)S(1)}, u32[]{:S(2)}, u32[]{:S(2)}) collective-permute-start(bf16[2,128,256]{2,1,0:T(8,128)(2,1)S(1)} %get-tuple-element.35), channel_id=1, source_target_pairs={{0,8},{2,10},{4,12},{6,14},{8,0},{10,2},{12,4},{14,6},{1,9},{3,11}... | collective-permute-start | bytes 393224 | tf_op jit(solution)/shard_map/ppermute | solution.py:37
  67.2 7.6 %collective-permute-start.19 = (bf16[2,128,256]{2,1,0:T(8,128)(2,1)S(1)}, bf16[2,128,256]{2,1,0:T(8,128)(2,1)S(1)}, u32[]{:S(2)}, u32[]{:S(2)}) collective-permute-start(bf16[2,128,256]{2,1,0:T(8,128)(2,1)S(1)} %get-tuple-element.36), channel_id=1, source_target_pairs={{0,12},{2,14},{4,8},{6,10},{8,4},{10,6},{12,0},{14,2},{1,13},{3,15... | collective-permute-start | bytes 393224 | tf_op jit(solution)/shard_map/ppermute | solution.py:37
  75.7 8.3 %collective-permute-start.27 = (bf16[2,256,128]{2,1,0:T(8,128)(2,1)S(1)}, bf16[2,256,128]{2,1,0:T(8,128)(2,1)S(1)}, u32[]{:S(2)}, u32[]{:S(2)}) collective-permute-start(bf16[2,256,128]{2,1,0:T(8,128)(2,1)S(1)} %get-tuple-element.38.rest_0_), channel_id=1, source_target_pairs={{0,1},{1,0},{2,3},{3,2},{4,5},{5,4},{6,7},{7,6},{8,9},{9,8},{10,11... | collective-permute-start | bytes 393224 | tf_op jit(solution)/shard_map/ppermute | solution.py:29
  75.8 8.4 %collective-permute-start.26 = (bf16[2,256,128]{2,1,0:T(8,128)(2,1)S(1)}, bf16[2,256,128]{2,1,0:T(8,128)(2,1)S(1)}, u32[]{:S(2)}, u32[]{:S(2)}) collective-permute-start(bf16[2,256,128]{2,1,0:T(8,128)(2,1)S(1)} %get-tuple-element.38.rest_0_), channel_id=1, source_target_pairs={{0,12},{2,14},{4,8},{6,10},{8,4},{10,6},{12,0},{14,2},{1,13},{3,15... | collective-permute-start | bytes 393224 | tf_op jit(solution)/shard_map/ppermute | solution.py:37
  78.4 8.7 %collective-permute-start.25 = (bf16[2,256,128]{2,1,0:T(8,128)(2,1)S(1)}, bf16[2,256,128]{2,1,0:T(8,128)(2,1)S(1)}, u32[]{:S(2)}, u32[]{:S(2)}) collective-permute-start(bf16[2,256,128]{2,1,0:T(8,128)(2,1)S(1)} %get-tuple-element.38.rest_0_), channel_id=1, source_target_pairs={{0,8},{2,10},{4,12},{6,14},{8,0},{10,2},{12,4},{14,6},{1,9},{3,11}... | collective-permute-start | bytes 393224 | tf_op jit(solution)/shard_map/ppermute | solution.py:37
  79.1 14.5 %collective-permute-start.24 = (bf16[2,256,128]{2,1,0:T(8,128)(2,1)S(1)}, bf16[2,256,128]{2,1,0:T(8,128)(2,1)S(1)}, u32[]{:S(2)}, u32[]{:S(2)}) collective-permute-start(bf16[2,256,128]{2,1,0:T(8,128)(2,1)S(1)} %get-tuple-element.38.rest_0_), channel_id=1, source_target_pairs={{0,4},{2,6},{4,0},{6,2},{8,12},{10,14},{12,8},{14,10},{1,5},{3,7},... | collective-permute-start | bytes 393224 | tf_op jit(solution)/shard_map/ppermute | solution.py:37
  80.8 12.8 %collective-permute-start.23 = (bf16[2,256,128]{2,1,0:T(8,128)(2,1)S(1)}, bf16[2,256,128]{2,1,0:T(8,128)(2,1)S(1)}, u32[]{:S(2)}, u32[]{:S(2)}) collective-permute-start(bf16[2,256,128]{2,1,0:T(8,128)(2,1)S(1)} %get-tuple-element.38.rest_0_), channel_id=1, source_target_pairs={{0,14},{2,8},{4,10},{6,12},{8,6},{10,0},{12,2},{14,4},{1,15},{3,9}... | collective-permute-start | bytes 393224 | tf_op jit(solution)/shard_map/ppermute | solution.py:37
  84.0 10.1 %collective-permute-start.22 = (bf16[2,256,128]{2,1,0:T(8,128)(2,1)S(1)}, bf16[2,256,128]{2,1,0:T(8,128)(2,1)S(1)}, u32[]{:S(2)}, u32[]{:S(2)}) collective-permute-start(bf16[2,256,128]{2,1,0:T(8,128)(2,1)S(1)} %get-tuple-element.38.rest_0_), channel_id=1, source_target_pairs={{0,6},{2,0},{4,2},{6,4},{8,14},{10,8},{12,10},{14,12},{1,7},{3,1},... | collective-permute-start | bytes 393224 | tf_op jit(solution)/shard_map/ppermute | solution.py:37
  84.2 10.0 %collective-permute-start.21 = (bf16[2,256,128]{2,1,0:T(8,128)(2,1)S(1)}, bf16[2,256,128]{2,1,0:T(8,128)(2,1)S(1)}, u32[]{:S(2)}, u32[]{:S(2)}) collective-permute-start(bf16[2,256,128]{2,1,0:T(8,128)(2,1)S(1)} %get-tuple-element.38.rest_0_), channel_id=1, source_target_pairs={{0,10},{2,12},{4,14},{6,8},{8,2},{10,4},{12,6},{14,0},{1,11},{3,13... | collective-permute-start | bytes 393224 | tf_op jit(solution)/shard_map/ppermute | solution.py:37
  87.1 9.0 %collective-permute-start.20 = (bf16[2,256,128]{2,1,0:T(8,128)(2,1)S(1)}, bf16[2,256,128]{2,1,0:T(8,128)(2,1)S(1)}, u32[]{:S(2)}, u32[]{:S(2)}) collective-permute-start(bf16[2,256,128]{2,1,0:T(8,128)(2,1)S(1)} %get-tuple-element.38.rest_0_), channel_id=1, source_target_pairs={{0,2},{2,4},{4,6},{6,0},{8,10},{10,12},{12,14},{14,8},{1,3},{3,5},... | collective-permute-start | bytes 393224 | tf_op jit(solution)/shard_map/ppermute | solution.py:37
  107.3 9.6 %collective-permute-start.35 = (bf16[1,2,256,128]{3,2,1,0:T(8,128)(2,1)S(1)}, bf16[1,2,256,128]{3,2,1,0:T(8,128)(2,1)S(1)}, u32[]{:S(2)}, u32[]{:S(2)}) collective-permute-start(bf16[1,2,256,128]{3,2,1,0:T(8,128)(2,1)S(1)} %get-tuple-element.42), channel_id=1, source_target_pairs={{0,128},{128,0},{1,129},{129,1},{2,130},{130,2},{3,131},{131,3},{4... | collective-permute-start | bytes 393224 | tf_op jit(solution)/shard_map/ppermute | solution.py:29
  114.0 9.6 %collective-permute-start.38 = (bf16[2,2,256,128]{3,2,1,0:T(8,128)(2,1)S(1)}, bf16[2,2,256,128]{3,2,1,0:T(8,128)(2,1)S(1)}, u32[]{:S(2)}, u32[]{:S(2)}) collective-permute-start(bf16[2,2,256,128]{3,2,1,0:T(8,128)(2,1)S(1)} %get-tuple-element.47), channel_id=1, source_target_pairs={{0,128},{128,0},{1,129},{129,1},{2,130},{130,2},{3,131},{131,3},{4... | collective-permute-start | bytes 786440 | tf_op jit(solution)/shard_map/ppermute | solution.py:29
  116.9 7.0 %collective-permute-start.40 = (bf16[2,256,128]{2,1,0:T(8,128)(2,1)S(1)}, bf16[2,256,128]{2,1,0:T(8,128)(2,1)S(1)}, u32[]{:S(2)}, u32[]{:S(2)}) collective-permute-start(bf16[2,256,128]{2,1,0:T(8,128)(2,1)S(1)} %fusion.5), channel_id=1, source_target_pairs={{0,16},{16,32},{32,48},{48,64},{64,80},{80,96},{96,112},{112,0},{1... | collective-permute-start | bytes 393224 | tf_op jit(solution)/shard_map/ppermute | solution.py:25
  118.3 11.0 %collective-permute-start.36 = (bf16[2,2,256,128]{3,2,1,0:T(8,128)(2,1)S(1)}, bf16[2,2,256,128]{3,2,1,0:T(8,128)(2,1)S(1)}, u32[]{:S(2)}, u32[]{:S(2)}) collective-permute-start(bf16[2,2,256,128]{3,2,1,0:T(8,128)(2,1)S(1)} %get-tuple-element.43), channel_id=1, source_target_pairs={{0,128},{128,0},{1,129},{129,1},{2,130},{130,2},{3,131},{131,3},{4... | collective-permute-start | bytes 786440 | tf_op jit(solution)/shard_map/ppermute | solution.py:29
  124.0 6.8 %collective-permute-start.41 = (bf16[2,256,128]{2,1,0:T(8,128)(2,1)S(1)}, bf16[2,256,128]{2,1,0:T(8,128)(2,1)S(1)}, u32[]{:S(2)}, u32[]{:S(2)}) collective-permute-start(bf16[2,256,128]{2,1,0:T(8,128)(2,1)S(1)} %fusion.2), channel_id=1, source_target_pairs={{0,16},{16,32},{32,48},{48,64},{64,80},{80,96},{96,112},{112,0},{1... | collective-permute-start | bytes 393224 | tf_op jit(solution)/shard_map/ppermute | solution.py:25
  125.9 9.4 %collective-permute-start.39 = (bf16[2,2,256,128]{3,2,1,0:T(8,128)(2,1)S(1)}, bf16[2,2,256,128]{3,2,1,0:T(8,128)(2,1)S(1)}, u32[]{:S(2)}, u32[]{:S(2)}) collective-permute-start(bf16[2,2,256,128]{3,2,1,0:T(8,128)(2,1)S(1)} %get-tuple-element.48), channel_id=1, source_target_pairs={{0,128},{128,0},{1,129},{129,1},{2,130},{130,2},{3,131},{131,3},{4... | collective-permute-start | bytes 786440 | tf_op jit(solution)/shard_map/ppermute | solution.py:29
  133.1 6.2 %collective-permute-start.42 = (bf16[2,256,128]{2,1,0:T(8,128)(2,1)S(1)}, bf16[2,256,128]{2,1,0:T(8,128)(2,1)S(1)}, u32[]{:S(2)}, u32[]{:S(2)}) collective-permute-start(bf16[2,256,128]{2,1,0:T(8,128)(2,1)S(1)} %get-tuple-element.55), channel_id=1, source_target_pairs={{0,16},{16,32},{32,48},{48,64},{64,80},{80,96},{96,112},{112,0},{1... | collective-permute-start | bytes 393224 | tf_op jit(solution)/shard_map/ppermute | solution.py:25
  133.1 8.7 %collective-permute-start.37 = (bf16[1,2,256,128]{3,2,1,0:T(8,128)(2,1)S(1)}, bf16[1,2,256,128]{3,2,1,0:T(8,128)(2,1)S(1)}, u32[]{:S(2)}, u32[]{:S(2)}) collective-permute-start(bf16[1,2,256,128]{3,2,1,0:T(8,128)(2,1)S(1)} %get-tuple-element.44), channel_id=1, source_target_pairs={{0,128},{128,0},{1,129},{129,1},{2,130},{130,2},{3,131},{131,3},{4... | collective-permute-start | bytes 393224 | tf_op jit(solution)/shard_map/ppermute | solution.py:29
  141.8 7.4 %collective-permute-start.43 = (bf16[2,256,128]{2,1,0:T(8,128)(2,1)S(1)}, bf16[2,256,128]{2,1,0:T(8,128)(2,1)S(1)}, u32[]{:S(2)}, u32[]{:S(2)}) collective-permute-start(bf16[2,256,128]{2,1,0:T(8,128)(2,1)S(1)} %get-tuple-element.53), channel_id=1, source_target_pairs={{0,16},{16,32},{32,48},{48,64},{64,80},{80,96},{96,112},{112,0},{1... | collective-permute-start | bytes 393224 | tf_op jit(solution)/shard_map/ppermute | solution.py:25
  (30 other events, 251.1 us)
